TPU v7x, 32 devices: a whole 2x2x4 slice. The times are simulated.
32 devices in a mesh: pipe: 2 (over core), expert: 4 (over z), dp: 4 (over y, x).
Axes of the slice: x: 2, y: 2, z: 4, core: 2. Of those that a mesh axis runs over, the one named last changes fastest.
Arguments:
- tokens: bfloat16 [2, 128, 3584], P('pipe', ('expert', 'dp')), may hold values from -6 to 6
- grad_out: bfloat16 [2, 128, 3584], P('pipe', ('expert', 'dp')), may hold values from -1.5 to 1.5
- routes: int32 [2, 128, 1], P('pipe', ('expert', 'dp')), may hold values from 0 to 1; in each aligned block of 8 rows (0 to 7, 8 to 15, ..., all dimensions but the last counted through in order) at most 6 rows name the same one
- combine: bfloat16 [2, 128, 1], P('pipe', ('expert', 'dp')), may hold values from 0.25 to 2.5
- w_gate: bfloat16 [2, 3584, 512], P('pipe', 'dp', 'expert'), may hold values from -0.09375 to 0.09375
- w_up: bfloat16 [2, 3584, 512], P('pipe', 'dp', 'expert'), may hold values from -0.09375 to 0.09375
- w_down: bfloat16 [2, 3584, 512], P('pipe', 'dp', 'expert'), may hold values from -0.375 to 0.375
Outputs:
- passed: bfloat16 [2, 128, 3584], P('pipe', ('expert', 'dp'))
- grad_combine: float32 [2, 128, 1], P('pipe', ('expert', 'dp'))
- grad_gate: float32 [2, 3584, 512], P('pipe', 'dp', 'expert')
- grad_up: float32 [2, 3584, 512], P('pipe', 'dp', 'expert')
- grad_down: float32 [2, 3584, 512], P('pipe', 'dp', 'expert')
Inputs may be any that keep to these rules, and one draw needn't show every extreme that they name: `routes`: each token names 1 different experts; among the 8 tokens of one device no expert is named more than 6 times, and in some device's tokens an expert is named exactly 6 times.
All inputs are finite; a program needn't handle non-finite values.
Results may differ from a plain program's by a relative error of at most 0.012.
Values may be sent and summed in bfloat16 or wider, within the bound.
A program may use at most 128 MiB of HBM per device.

v0:
```python
import jax
import jax.numpy as jnp
from jax import lax
from jax.sharding import PartitionSpec as P

contract_last = (((1,), (1,)), ((), ()))
contract_first = (((0,), (0,)), ((), ()))


def from_behind(block, axis, distance):
    devices = range(lax.axis_size(axis))
    route = [((i - distance) % len(devices), i) for i in devices]
    return lax.ppermute(block, axis, route)


def activate(gate_pre, up_pre):
    sigmoid_gate = jax.nn.sigmoid(gate_pre)
    activated = gate_pre * sigmoid_gate
    hidden = (activated * up_pre).astype(jnp.bfloat16)
    return (sigmoid_gate, activated, hidden)


def backprop_hidden(hidden_grad, gate_pre, up_pre, sigmoid_gate, activated):
    gate_grad = (
        hidden_grad * up_pre * sigmoid_gate * (1.0 + gate_pre * (1.0 - sigmoid_gate))
    ).astype(jnp.bfloat16)
    up_grad = (hidden_grad * activated).astype(jnp.bfloat16)
    return (gate_grad, up_grad)


def body(tokens, grad_out, routes, combine, w_gate, w_up, w_down):
    model_width = tokens.shape[2]
    tok_count = tokens.shape[1]
    top_count = routes.shape[2]
    hidden_dev = w_gate.shape[2]
    devices = lax.axis_size("expert")
    slices = min(8, devices // 2)
    expert_count = devices // slices
    capacity = min(tok_count, max(2, 3 * tok_count * top_count // (2 * expert_count)))
    slot_count = expert_count * capacity
    flat_routes = routes[0].reshape(-1)
    onehot = (flat_routes[:, None] == jnp.arange(expert_count, dtype=jnp.int32)[None, :]).astype(
        jnp.int32
    )
    earlier = jnp.cumsum(onehot, axis=0) - onehot
    position = jnp.sum(earlier * onehot, axis=1)
    slot_of = flat_routes * capacity + position
    placed = slot_of[None, :] == jnp.arange(slot_count, dtype=jnp.int32)[:, None]
    placed_float = placed.astype(jnp.float32)
    owner_mask = jnp.any(placed.reshape(slot_count, tok_count, top_count), axis=2)
    owner_half = owner_mask.astype(jnp.bfloat16)
    slot_inputs = jnp.dot(owner_half, tokens[0], preferred_element_type=jnp.float32).astype(
        jnp.bfloat16
    )
    slot_cotangent = jnp.dot(owner_half, grad_out[0], preferred_element_type=jnp.float32).astype(
        jnp.bfloat16
    )
    slot_weight = jnp.dot(
        placed.astype(jnp.bfloat16), combine[0].reshape(-1), preferred_element_type=jnp.float32
    ).astype(jnp.bfloat16)

    def replicate_slots(array):
        tail_shape = array.shape[1:]
        shaped = array.reshape((expert_count, 1, capacity) + tail_shape)
        spread = jnp.broadcast_to(shaped, (expert_count, slices, capacity) + tail_shape)
        return spread.reshape((devices, capacity) + tail_shape)

    got_inputs, got_cotangent, got_weight = (
        lax.all_to_all(
            replicate_slots(slot_inputs), "expert", split_axis=0, concat_axis=0, tiled=True
        ),
        lax.all_to_all(
            replicate_slots(slot_cotangent), "expert", split_axis=0, concat_axis=0, tiled=True
        ),
        lax.all_to_all(
            replicate_slots(slot_weight), "expert", split_axis=0, concat_axis=0, tiled=True
        ),
    )
    row_count = devices * capacity
    row_inputs = got_inputs.reshape(row_count, model_width)
    row_cotangent = got_cotangent.reshape(row_count, model_width)
    row_weight = got_weight.reshape(row_count).astype(jnp.float32)
    out_grad = (row_weight[:, None] * row_cotangent.astype(jnp.float32)).astype(jnp.bfloat16)
    full_gate, full_up, full_down = (
        lax.all_gather(w_gate, "dp", axis=1, tiled=True),
        lax.all_gather(w_up, "dp", axis=1, tiled=True),
        lax.all_gather(w_down, "dp", axis=1, tiled=True),
    )
    gate_mat = full_gate[0]
    up_mat = full_up[0]
    down_mat = full_down[0]
    gate_pre = jnp.dot(row_inputs, gate_mat, preferred_element_type=jnp.float32)
    up_pre = jnp.dot(row_inputs, up_mat, preferred_element_type=jnp.float32)
    sigmoid_gate, activated, hidden = activate(gate_pre, up_pre)
    expert_out = lax.dot_general(
        hidden, down_mat, contract_last, preferred_element_type=jnp.float32
    )
    hidden_grad = jnp.dot(out_grad, down_mat, preferred_element_type=jnp.float32)
    gate_grad, up_grad = backprop_hidden(hidden_grad, gate_pre, up_pre, sigmoid_gate, activated)
    input_rows = lax.dot_general(
        gate_grad, gate_mat, contract_last, preferred_element_type=jnp.float32
    )
    input_rows = input_rows + lax.dot_general(
        up_grad, up_mat, contract_last, preferred_element_type=jnp.float32
    )
    route_score = jnp.sum(expert_out * row_cotangent.astype(jnp.float32), axis=1)
    back_rows, back_score = (
        lax.all_to_all(
            input_rows.reshape(devices, capacity, model_width).astype(jnp.bfloat16),
            "expert",
            split_axis=0,
            concat_axis=0,
            tiled=True,
        ).astype(jnp.float32),
        lax.all_to_all(
            route_score.reshape(devices, capacity).astype(jnp.bfloat16),
            "expert",
            split_axis=0,
            concat_axis=0,
            tiled=True,
        ).astype(jnp.float32),
    )
    slot_grad = jnp.sum(back_rows.reshape(expert_count, slices, capacity, model_width), axis=1)
    slot_grad = slot_grad.reshape(slot_count, model_width)
    slot_score = jnp.sum(back_score.reshape(expert_count, slices, capacity), axis=1).reshape(
        slot_count
    )
    token_grad = lax.dot_general(
        owner_mask.astype(jnp.float32),
        slot_grad,
        contract_first,
        precision=lax.Precision.HIGHEST,
        preferred_element_type=jnp.float32,
    )
    route_grad = lax.dot_general(
        placed_float,
        slot_score,
        contract_first,
        precision=lax.Precision.HIGHEST,
        preferred_element_type=jnp.float32,
    )
    passed = from_behind(token_grad.astype(jnp.bfloat16)[None], "pipe", -1)
    shares = lax.psum_scatter(
        jnp.concatenate(
            [
                lax.dot_general(
                    row_inputs, gate_grad, contract_first, preferred_element_type=jnp.float32
                ),
                lax.dot_general(
                    row_inputs, up_grad, contract_first, preferred_element_type=jnp.float32
                ),
                lax.dot_general(
                    out_grad, hidden, contract_first, preferred_element_type=jnp.float32
                ),
            ],
            axis=1,
        ).astype(jnp.bfloat16),
        "dp",
        scatter_dimension=0,
        tiled=True,
    ).astype(jnp.float32)
    grad_gate = shares[:, :hidden_dev][None]
    grad_up = shares[:, hidden_dev : 2 * hidden_dev][None]
    grad_down = shares[:, 2 * hidden_dev :][None]
    return (passed, route_grad.reshape(1, tok_count, top_count), grad_gate, grad_up, grad_down)


def solution(mesh):
    in_specs = (
        P("pipe", ("expert", "dp"), None),
        P("pipe", ("expert", "dp"), None),
        P("pipe", ("expert", "dp"), None),
        P("pipe", ("expert", "dp"), None),
        P("pipe", "dp", "expert"),
        P("pipe", "dp", "expert"),
        P("pipe", "dp", "expert"),
    )
    out_specs = (
        P("pipe", ("expert", "dp"), None),
        P("pipe", ("expert", "dp"), None),
        P("pipe", "dp", "expert"),
        P("pipe", "dp", "expert"),
        P("pipe", "dp", "expert"),
    )
    return jax.shard_map(body, mesh=mesh, in_specs=in_specs, out_specs=out_specs, check_vma=False)
```

profile of v0, /device:TPU:1, one launch (start us, length us, event | category | flops | bytes accessed | tf_op | source)
XLA Modules:
  0.0 133.8 jit_solution(12448290919742431956)
XLA Ops:
  7.2 0.7 fusion.23
  7.9 0.2 reduce_window_sum.11
  8.1 0.7 select_reduce_fusion
  8.8 0.7 multiply_add_fusion
  9.4 0.8 fusion.3
  10.3 0.6 copy.23
  10.9 5.4 %all-to-all-start = ((bf16[4,1,6]{2,1,0:T(2,128)(2,1)}), bf16[4,1,6]{2,1,0:T(2,128)(2,1)S(1)}, u32[]{:S(2)}, u32[]{:S(2)}) async-start(bf16[4,1,6]{2,1,0:T(2,128)(2,1)} %copy.23), calls=%async_computation | async-start | bytes 4096 | tf_op jit(solution)/shard_map/all_to_all | solution.py:75
  16.3 0.2 convolution_convert_fusion.3
  16.5 1.0 convolution_convert_fusion.4
  17.5 11.6 %all_gather.11 = bf16[1,3584,128]{2,1,0:T(8,128)(2,1)S(1)} all-gather(bf16[1,896,128]{2,1,0:T(8,128)(2,1)} %param.11), channel_id=1, replica_groups=mesh['pipe'=2,'expert'=4,'dp'=4] {'dp'}, dimensions={1}, use_global_device_ids=true | all-gather | bytes 1146880 | tf_op jit(solution)/shard_map/all_gather | solution.py:85
  29.1 10.1 %all_gather.10 = bf16[1,3584,128]{2,1,0:T(8,128)(2,1)S(1)} all-gather(bf16[1,896,128]{2,1,0:T(8,128)(2,1)} %param.12), channel_id=1, replica_groups=mesh['pipe'=2,'expert'=4,'dp'=4] {'dp'}, dimensions={1}, use_global_device_ids=true | all-gather | bytes 1146880 | tf_op jit(solution)/shard_map/all_gather | solution.py:86
  39.2 0.8 broadcast_in_dim.40
  40.0 4.5 %all-to-all-start.1 = ((bf16[4,6,3584]{2,1,0:T(8,128)(2,1)}), bf16[4,6,3584]{2,1,0:T(8,128)(2,1)S(1)}, u32[]{:S(2)}, u32[]{:S(2)}) async-start(bf16[4,6,3584]{2,1,0:T(8,128)(2,1)} %bitcast.7), calls=%async_computation.1 | async-start | bytes 458752 | tf_op jit(solution)/shard_map/all_to_all | solution.py:72
  44.5 9.5 %all_gather.9 = bf16[1,3584,128]{2,1,0:T(8,128)(2,1)S(1)} all-gather(bf16[1,896,128]{2,1,0:T(8,128)(2,1)S(1)} %copy-done.7), channel_id=1, replica_groups=mesh['pipe'=2,'expert'=4,'dp'=4] {'dp'}, dimensions={1}, use_global_device_ids=true | all-gather | bytes 1146880 | tf_op jit(solution)/shard_map/all_gather | solution.py:87
  54.0 0.7 reshape.110
  54.7 0.7 broadcast_in_dim.42
  55.4 4.2 %all-to-all-start.2 = ((bf16[4,6,3584]{2,1,0:T(8,128)(2,1)}), bf16[4,6,3584]{2,1,0:T(8,128)(2,1)}, u32[]{:S(2)}, u32[]{:S(2)}) async-start(bf16[4,6,3584]{2,1,0:T(8,128)(2,1)} %bitcast.10), calls=%async_computation.2 | async-start | bytes 458752 | tf_op jit(solution)/shard_map/all_to_all | solution.py:69
  59.6 0.1 multiply_convert_fusion
  59.8 5.3 %all-to-all-done.2 = bf16[4,6,3584]{2,1,0:T(8,128)(2,1)} async-done(((bf16[4,6,3584]{2,1,0:T(8,128)(2,1)}), bf16[4,6,3584]{2,1,0:T(8,128)(2,1)}, u32[]{:S(2)}, u32[]{:S(2)}) %all-to-all-start.2) | async-done | bytes 172064 | tf_op jit(solution)/shard_map/all_to_all | solution.py:69
  65.1 1.0 reshape.99
  66.1 0.2 fusion.6
  66.4 0.2 fusion.12
  66.6 0.3 multiply_convert_fusion.3
  66.9 1.4 %convolution_convert_fusion.2 = bf16[3584,128]{0,1:T(8,128)(2,1)} fusion(bf16[24,3584]{1,0:T(8,128)(2,1)S(1)} %reshape.99, bf16[24,128]{1,0:T(8,128)(2,1)S(1)} %get-tuple-element.29), kind=kOutput, calls=%fused_computation.2 | convolution fusion | flops 22478848 | bytes 1095680 | tf_op jit(solution)/shard_map/dot_general | solution.py:146
  68.3 1.4 %convolution_convert_fusion.1 = bf16[3584,128]{0,1:T(8,128)(2,1)} fusion(bf16[24,3584]{1,0:T(8,128)(2,1)S(1)} %reshape.99, bf16[24,128]{1,0:T(8,128)(2,1)S(1)} %get-tuple-element.30), kind=kOutput, calls=%fused_computation.1 | convolution fusion | flops 22478848 | bytes 1095680 | tf_op jit(solution)/shard_map/dot_general | solution.py:149
  69.8 0.5 convolution_convert_fusion
  70.2 1.6 %pad_maximum_fusion = bf16[3584,384]{0,1:T(8,128)(2,1)S(1)} fusion(bf16[3584,128]{0,1:T(8,128)(2,1)S(1)} %convolution_convert_fusion, bf16[3584,128]{0,1:T(8,128)(2,1)} %convolution_convert_fusion.1, bf16[3584,128]{0,1:T(8,128)(2,1)} %convolution_convert_fusion.2), kind=kLoop, calls=%fused_computation.10 | loop fusion | flops 8257536 | bytes 5505024 | tf_op jit(solution)/shard_map/concatenate | solution.py:144
  71.9 2.7 %copy.28 = bf16[3584,384]{1,0:T(8,128)(2,1)} copy(bf16[3584,384]{0,1:T(8,128)(2,1)S(1)} %pad_maximum_fusion) | data formatting | bytes 5505024
  74.7 1.1 copy-done.6
  75.8 0.7 fusion.2
  76.5 0.7 convert_element_type.126
  77.2 3.2 %all-to-all-start.4 = ((bf16[4,1,6]{2,1,0:T(2,128)(2,1)}), bf16[4,1,6]{2,1,0:T(2,128)(2,1)S(1)}, u32[]{:S(2)}, u32[]{:S(2)}) async-start(bf16[4,1,6]{2,1,0:T(2,128)(2,1)} %convert_element_type.126), calls=%async_computation.4 | async-start | bytes 4096 | tf_op jit(solution)/shard_map/all_to_all | solution.py:115
  80.4 0.6 fusion.4
  81.0 0.6 fusion
  81.6 0.8 convert_element_type.109
  82.4 2.3 %all-to-all-done.4 = bf16[4,1,6]{2,1,0:T(2,128)(2,1)S(1)} async-done(((bf16[4,1,6]{2,1,0:T(2,128)(2,1)}), bf16[4,1,6]{2,1,0:T(2,128)(2,1)S(1)}, u32[]{:S(2)}, u32[]{:S(2)}) %all-to-all-start.4) | async-done | bytes 80 | tf_op jit(solution)/shard_map/all_to_all | solution.py:115
  84.7 3.4 %all-to-all-start.3 = ((bf16[4,6,3584]{2,1,0:T(8,128)(2,1)}), bf16[4,6,3584]{2,1,0:T(8,128)(2,1)S(1)}, u32[]{:S(2)}, u32[]{:S(2)}) async-start(bf16[4,6,3584]{2,1,0:T(8,128)(2,1)} %convert_element_type.109), calls=%async_computation.3 | async-start | bytes 458752 | tf_op jit(solution)/shard_map/all_to_all | solution.py:108
  88.2 5.5 %all-to-all-done.3 = bf16[4,6,3584]{2,1,0:T(8,128)(2,1)S(1)} async-done(((bf16[4,6,3584]{2,1,0:T(8,128)(2,1)}), bf16[4,6,3584]{2,1,0:T(8,128)(2,1)S(1)}, u32[]{:S(2)}, u32[]{:S(2)}) %all-to-all-start.3) | async-done | bytes 172064 | tf_op jit(solution)/shard_map/all_to_all | solution.py:108
  93.8 0.3 fusion.1
  94.1 10.5 %collective-permute-start = (bf16[1,8,3584]{2,1,0:T(8,128)(2,1)S(1)}, bf16[1,8,3584]{2,1,0:T(8,128)(2,1)S(1)}, u32[]{:S(2)}, u32[]{:S(2)}) collective-permute-start(bf16[1,8,3584]{2,1,0:T(8,128)(2,1)S(1)} %fusion.1), channel_id=1, source_target_pairs={{16,0},{0,16},{17,1},{1,17},{18,2},{2,18},{19,3},{3,19},{20,4},{4,... | collective-permute-start | bytes 172040 | tf_op jit(solution)/shard_map/ppermute | solution.py:13
  104.5 0.6 convolution_bitcast_fusion
  105.2 0.2 collective-permute-done
  105.4 16.4 %reduce-scatter.4.cloned.1.call-done = bf16[896,384]{1,0:T(8,128)(2,1)} async-done(((bf16[3584,384]{1,0:T(8,128)(2,1)}), bf16[896,384]{1,0:T(8,128)(2,1)}) %reduce-scatter.4.cloned.1.call-update) | async-done | bytes 688144
  121.8 1.4 %copy.29 = bf16[896,384]{0,1:T(8,128)(2,1)S(1)} copy(bf16[896,384]{1,0:T(8,128)(2,1)} %reduce-scatter.4.cloned.1.call-done) | data formatting | bytes 1376256
  123.4 1.0 copy.27
  124.4 1.0 copy.26
  125.4 1.0 copy.25
  126.3 0.6 copy.31
  (40 shorter events, 0.7 us)
Async XLA Ops:
  7.2 9.1 %copy-start = (bf16[1,8,3584]{2,1,0:T(8,128)(2,1)S(1)}, bf16[1,8,3584]{2,1,0:T(8,128)(2,1)}, u32[]{:S(2)}) copy-start(bf16[1,8,3584]{2,1,0:T(8,128)(2,1)} %param.7) | copy-start | bytes 172036
  7.2 37.3 %copy-start.7 = (bf16[1,896,128]{2,1,0:T(8,128)(2,1)S(1)}, bf16[1,896,128]{2,1,0:T(8,128)(2,1)}, u32[]{:S(2)}) copy-start(bf16[1,896,128]{2,1,0:T(8,128)(2,1)} %param.13) | copy-start | bytes 688132
  9.4 30.6 %copy-start.8 = (s32[8]{0:T(128)}, s32[8]{0:T(128)S(1)}, u32[]{:S(2)}) copy-start(s32[8]{0:T(128)S(1)} %multiply_add_fusion) | copy-start | bytes 100
  10.9 28.3 %all-to-all-start = ((bf16[4,1,6]{2,1,0:T(2,128)(2,1)}), bf16[4,1,6]{2,1,0:T(2,128)(2,1)S(1)}, u32[]{:S(2)}, u32[]{:S(2)}) async-start(bf16[4,1,6]{2,1,0:T(2,128)(2,1)} %copy.23), calls=%async_computation | async-start | bytes 4096 | tf_op jit(solution)/shard_map/all_to_all | solution.py:75
  29.1 37.3 %copy-start.1 = (bf16[1,3584,128]{2,1,0:T(8,128)(2,1)}, bf16[1,3584,128]{2,1,0:T(8,128)(2,1)S(1)}, u32[]{:S(2)}) copy-start(bf16[1,3584,128]{2,1,0:T(8,128)(2,1)S(1)} %all_gather.11) | copy-start | bytes 2752516
  39.2 27.5 %copy-start.3 = (bf16[1,3584,128]{2,1,0:T(8,128)(2,1)}, bf16[1,3584,128]{2,1,0:T(8,128)(2,1)S(1)}, u32[]{:S(2)}) copy-start(bf16[1,3584,128]{2,1,0:T(8,128)(2,1)S(1)} %all_gather.10) | copy-start | bytes 2752516
  40.0 14.7 %all-to-all-start.1 = ((bf16[4,6,3584]{2,1,0:T(8,128)(2,1)}), bf16[4,6,3584]{2,1,0:T(8,128)(2,1)S(1)}, u32[]{:S(2)}, u32[]{:S(2)}) async-start(bf16[4,6,3584]{2,1,0:T(8,128)(2,1)} %bitcast.7), calls=%async_computation.1 | async-start | bytes 458752 | tf_op jit(solution)/shard_map/all_to_all | solution.py:72
  54.0 14.4 %copy-start.5 = (bf16[1,3584,128]{2,1,0:T(8,128)(2,1)}, bf16[1,3584,128]{2,1,0:T(8,128)(2,1)S(1)}, u32[]{:S(2)}) copy-start(bf16[1,3584,128]{2,1,0:T(8,128)(2,1)S(1)} %all_gather.9) | copy-start | bytes 2752516
  55.4 9.7 %all-to-all-start.2 = ((bf16[4,6,3584]{2,1,0:T(8,128)(2,1)}), bf16[4,6,3584]{2,1,0:T(8,128)(2,1)}, u32[]{:S(2)}, u32[]{:S(2)}) async-start(bf16[4,6,3584]{2,1,0:T(8,128)(2,1)} %bitcast.10), calls=%async_computation.2 | async-start | bytes 458752 | tf_op jit(solution)/shard_map/all_to_all | solution.py:69
  59.6 62.2 %reduce-scatter.4.cloned.1.call-start = ((), (), s32[]{:S(2)}) async-start(), calls=%async_computation.6 | async-start | bytes 3440640
  66.6 3.1 %copy-start.10 = (f32[24]{0:T(128)S(1)}, f32[24]{0:T(128)}, u32[]{:S(2)}) copy-start(f32[24]{0:T(128)} %reshape.110) | copy-start | bytes 292
  74.6 1.2 copy-start.6
  74.6 5.8 %copy-start.2 = (bf16[1,3584,128]{2,1,0:T(8,128)(2,1)S(1)}, bf16[1,3584,128]{2,1,0:T(8,128)(2,1)}, u32[]{:S(2)}) copy-start(bf16[1,3584,128]{2,1,0:T(8,128)(2,1)} %copy-done.1) | copy-start | bytes 2752516
  74.6 6.4 %copy-start.4 = (bf16[1,3584,128]{2,1,0:T(8,128)(2,1)S(1)}, bf16[1,3584,128]{2,1,0:T(8,128)(2,1)}, u32[]{:S(2)}) copy-start(bf16[1,3584,128]{2,1,0:T(8,128)(2,1)} %copy-done.3) | copy-start | bytes 2752516
  75.8 18.0 %copy-start.9 = (s32[8]{0:T(128)S(1)}, s32[8]{0:T(128)}, u32[]{:S(2)}) copy-start(s32[8]{0:T(128)} %copy-done.8) | copy-start | bytes 100
  77.2 7.5 %all-to-all-start.4 = ((bf16[4,1,6]{2,1,0:T(2,128)(2,1)}), bf16[4,1,6]{2,1,0:T(2,128)(2,1)S(1)}, u32[]{:S(2)}, u32[]{:S(2)}) async-start(bf16[4,1,6]{2,1,0:T(2,128)(2,1)} %convert_element_type.126), calls=%async_computation.4 | async-start | bytes 4096 | tf_op jit(solution)/shard_map/all_to_all | solution.py:115
  84.7 9.0 %all-to-all-start.3 = ((bf16[4,6,3584]{2,1,0:T(8,128)(2,1)}), bf16[4,6,3584]{2,1,0:T(8,128)(2,1)S(1)}, u32[]{:S(2)}, u32[]{:S(2)}) async-start(bf16[4,6,3584]{2,1,0:T(8,128)(2,1)} %convert_element_type.109), calls=%async_computation.3 | async-start | bytes 458752 | tf_op jit(solution)/shard_map/all_to_all | solution.py:108
  94.1 11.4 %collective-permute-start = (bf16[1,8,3584]{2,1,0:T(8,128)(2,1)S(1)}, bf16[1,8,3584]{2,1,0:T(8,128)(2,1)S(1)}, u32[]{:S(2)}, u32[]{:S(2)}) collective-permute-start(bf16[1,8,3584]{2,1,0:T(8,128)(2,1)S(1)} %fusion.1), channel_id=1, source_target_pairs={{16,0},{0,16},{17,1},{1,17},{18,2},{2,18},{19,3},{3,19},{20,4},{4,... | collective-permute-start | bytes 172040 | tf_op jit(solution)/shard_map/ppermute | solution.py:13
Sparse Core Ops, SparseCore 0:
  74.8 46.9 reduce-scatter.3
where the time goes:
time: 135 us; the launch traced here: 134 us
  starting transfers between devices  31.2 us (23%)
  blocking collectives  31.2 us (23%)
  waiting for transfers between devices  29.8 us (22%)
  local copies, waits for them, and re-layouts  14.6 us (11%)
  between operations  14.2 us (11%)
  matrix products  8.69 us (6%)
  other arithmetic  4.14 us (3%)
    unnamed x2, waiting for transfers between devices  16.4 us
    all_gather x1, blocking collectives, body(): lax.all_gather(w_gate, 'dp', axis=1, tiled=True)  11.6 us
    ppermute x1, starting transfers between devices, from_behind(): return lax.ppermute(block, axis, route)  10.5 us
    all_gather x1, blocking collectives, body(): lax.all_gather(w_up, 'dp', axis=1, tiled=True)  10.1 us
    all_gather x1, blocking collectives, body(): lax.all_gather(w_down, 'dp', axis=1, tiled=True)  9.48 us
    unnamed x28, local copies, waits for them, and re-layouts  8.9 us
    all_to_all x1, waiting for transfers between devices, body(): lax.all_to_all(input_rows.reshape(devices, capacity, model_width).astype(...  5.52 us
    all_to_all x1, starting transfers between devices, body(): lax.all_to_all(replicate_slots(slot_weight), 'expert', split_axis=0, conc...  5.42 us
  transfers between devices with their start and end apart: 7, of which 5 were waited for; matrix products, arithmetic and copies ran while one was open for 5% of the time, Pallas kernels for 0%

commit v1 on v0

v1 whole, which is shorter than its diff:
```python
import functools

import jax
import jax.numpy as jnp
from jax import lax
from jax.experimental import pallas as pl
from jax.experimental.pallas import tpu as pltpu
from jax.sharding import PartitionSpec as P

MESH = pl.DeviceIdType.MESH
F32, BF16 = jnp.float32, jnp.bfloat16
contract_last = (((1,), (1,)), ((), ()))
contract_first = (((0,), (0,)), ((), ()))


def loop(count, step):
    if count <= 4:
        for i in range(count):
            step(i)
    else:
        pl.loop(0, count)(step)


def kernel(
    sizes, tok_ref, go_ref, routes_ref, comb_ref, wg_hbm, wu_hbm, wd_hbm,
    passed_ref, gc_ref, gg_ref, gu_ref, gd_ref,
    stage, xg, wcat, qbuf, hbuf, igsend, igrecv, ssend, srecv, fsend, frecv,
    wsem, p1s, gr, zs, qs, qr, igs, igr, ss, sr, fs, fr,
):
    pipes, E, DP, slices = sizes
    T = tok_ref.shape[1]
    top = routes_ref.shape[2]
    rows, hd = wg_hbm.shape[1:]
    pipe, e, d = (lax.axis_index(a) for a in ("pipe", "expert", "dp"))
    behind = lax.rem(pipe + pipes - 1, pipes)
    ahead = lax.rem(pipe + 1, pipes)
    my_expert = e // slices

    def peer(r):
        return lax.rem(d + r, DP)

    def other(r):
        return lax.rem(e + r, E)

    barrier = pltpu.get_barrier_semaphore()

    def greet(*who):
        pl.semaphore_signal(barrier, inc=1, device_id=who, device_id_type=MESH)

    loop(DP - 1, lambda r: greet(pipe, e, peer(r + 1)))
    loop(E - 1, lambda r: greet(pipe, other(r + 1), d))
    loop(DP, lambda r: greet(ahead, e, r))

    loads = [
        pltpu.make_async_copy(w.at[0], wcat.at[:, pl.ds(i * hd, hd)], wsem.at[i])
        for i, w in enumerate((wg_hbm, wu_hbm, wd_hbm))
    ]
    for c in loads:
        c.start()

    lane = lax.broadcasted_iota(jnp.int32, (T, 128), 1)
    weight = jnp.zeros((T, 128), F32)
    for k in range(top):
        weight = weight + jnp.where(
            routes_ref[0, :, k : k + 1] == lane, comb_ref[0, :, k : k + 1].astype(F32), 0.0
        )
    tail = jnp.concatenate([weight, jnp.zeros_like(weight)], axis=0).astype(BF16)
    for p in range(DP):
        both = jnp.concatenate(
            [
                tok_ref[0, :, p * rows : (p + 1) * rows].astype(F32),
                go_ref[0, :, p * rows : (p + 1) * rows].astype(F32),
            ],
            axis=0,
        ).astype(BF16)
        stage[p, :, :rows] = both
        stage[p, :, rows:] = tail

    pl.semaphore_wait(barrier, 2 * DP - 1 + E - 1)

    def remote(src, dst, send, recv, who):
        return pltpu.make_async_remote_copy(
            src_ref=src, dst_ref=dst, send_sem=send, recv_sem=recv,
            device_id=who, device_id_type=MESH,
        )

    def scatter(r):
        to = peer(r)
        return remote(stage.at[to], xg.at[e * DP + d], p1s.at[r], gr.at[e, d], (pipe, e, to))

    def relay(src, p, way):
        block = xg.at[src * DP + p]
        to = jnp.clip(e + (1 if way == 0 else -1), 0, E - 1)
        return remote(block, block, zs.at[way, src, p], gr.at[src, p], (pipe, to, d))

    def going(src, way):
        if way == 0:
            return jnp.logical_and(src <= e, e + 1 < E)
        return jnp.logical_and(src >= e, e > 0)

    def partial_to(src, r):
        block = qbuf.at[src * DP + d]
        return remote(block, block, qs.at[src, r], qr.at[src, d], (pipe, e, peer(r)))

    def partial_from(src, r):
        p = peer(r)
        block = qbuf.at[src * DP + p]
        return remote(block, block, qs.at[src, r], qr.at[src, p], (pipe, e, p))

    def rows_back(src):
        return remote(igsend.at[src], igrecv.at[e], igs.at[src], igr.at[e], (pipe, src, d))

    def score_back(src):
        return remote(ssend.at[src, d], srecv.at[e], ss.at[src], sr.at[e], (pipe, src, d))

    def rows_in(src):
        return remote(igsend.at[src], igrecv.at[src], igs.at[src], igr.at[src], (pipe, src, d))

    def score_in(src):
        return remote(ssend.at[src, d], srecv.at[src], ss.at[src], sr.at[src], (pipe, src, d))

    def hand_on(p):
        return remote(fsend.at[p], frecv.at[d], fs.at[p], fr.at[d], (behind, e, p))

    def handed(p):
        return remote(fsend.at[p], frecv.at[p], fs.at[p], fr.at[p], (behind, e, p))

    for r in range(1, DP):
        scatter(r).start()
    xg[e * DP + d] = stage[d]

    near = jnp.minimum(e, E - 1 - e)

    def source(i):
        half = (i + 1) // 2
        sign = jnp.where(i % 2 == 1, 1, -1)
        both_sides = e + sign * half
        one_side = jnp.where(e < E - 1 - e, e + (i - near), e - (i - near))
        return jnp.where(i <= 2 * near, both_sides, one_side)

    def arrive(i, first):
        src = e if first else source(i)
        for r in range(DP):
            p = peer(r)
            if not (first and r == 0):
                relay(src, p, 0).wait_recv()
            for way in range(2):
                @pl.when(going(src, way))
                def _():
                    relay(src, p, way).start()
        return src

    def project(src):
        block = xg[pl.ds(src * DP, DP)][:, :, :rows].reshape(DP * 2 * T, rows)
        part = jnp.dot(block, wcat[...], preferred_element_type=F32)
        part = part.reshape(DP, 2 * T, 3 * hd)
        q = jnp.concatenate([part[:, :T, : 2 * hd], part[:, T:, 2 * hd :]], axis=2)
        qbuf[src * DP + d] = q.reshape(DP * T, 3 * hd).astype(BF16)
        for r in range(1, DP):
            partial_to(src, r).start()

    def finish(src, own):
        for r in range(1, DP):
            partial_from(src, r).wait_recv()
        s = qbuf[src * DP].astype(F32)
        for p in range(1, DP):
            s = s + qbuf[src * DP + p].astype(F32)
        w = xg[pl.ds(src * DP, DP)][:, :, rows:].astype(F32)[:, :T].reshape(DP * T, 128)
        at = lax.broadcasted_iota(jnp.int32, (DP * T, 128), 1)
        g = jnp.sum(jnp.where(at == my_expert, w, 0.0), axis=1, keepdims=True)
        gate, up, hg = s[:, :hd], s[:, hd : 2 * hd], s[:, 2 * hd :]
        sig = jax.nn.sigmoid(gate)
        act = gate * sig
        hidden = jnp.where(g > 0.0, (act * up).astype(BF16).astype(F32), 0.0)
        hidden_grad = g * hg
        gate_grad = hidden_grad * up * sig * (1.0 + gate * (1.0 - sig))
        up_grad = hidden_grad * act
        score = jnp.sum(hidden * hg, axis=1, keepdims=True)
        ssend[src] = jnp.broadcast_to(score, (DP * T, 128)).reshape(DP, T, 128)
        both = jnp.concatenate([gate_grad, up_grad], axis=1)
        upper = jnp.concatenate([both, jnp.zeros_like(gate)], axis=1).reshape(DP, T, 3 * hd)
        lower = jnp.concatenate([jnp.zeros_like(both), g * hidden], axis=1).reshape(DP, T, 3 * hd)
        hbuf[pl.ds(src * DP, DP)] = jnp.concatenate([upper, lower], axis=1).astype(BF16)
        ig = lax.dot_general(
            both.astype(BF16), wcat[:, : 2 * hd], contract_last, preferred_element_type=F32
        ).astype(BF16)
        if own:
            igrecv[src] = ig
            srecv[src] = ssend[src, d]
        else:
            igsend[src] = ig
            rows_back(src).start()
            score_back(src).start()

    src = arrive(0, True)
    for c in loads:
        c.wait()
    project(src)
    last = src
    if E <= 4:
        for i in range(1, E):
            src = arrive(i, False)
            project(src)
            finish(last, i == 1)
            last = src
        finish(last, False)
    else:
        finish(src, True)

        @pl.loop(1, E)
        def _(i):
            src = arrive(i, False)
            project(src)
            finish(src, False)

    if E <= 4:
        a = xg[...][:, :, :rows].reshape(E * DP * 2 * T, rows)
        b = hbuf[...].reshape(E * DP * 2 * T, 3 * hd)
        grads = lax.dot_general(a, b, contract_first, preferred_element_type=F32)
        for i, ref in enumerate((gg_ref, gu_ref, gd_ref)):
            ref[0] = grads[:, i * hd : (i + 1) * hd]
    else:
        for ref in (gg_ref, gu_ref, gd_ref):
            ref[0] = jnp.zeros((rows, hd), F32)

        @pl.loop(0, E)
        def _(j):
            a = xg[pl.ds(j * DP, DP)][:, :, :rows].reshape(DP * 2 * T, rows)
            b = hbuf[pl.ds(j * DP, DP)].reshape(DP * 2 * T, 3 * hd)
            grads = lax.dot_general(a, b, contract_first, preferred_element_type=F32)
            for i, ref in enumerate((gg_ref, gu_ref, gd_ref)):
                ref[0] = ref[0] + grads[:, i * hd : (i + 1) * hd]

    def await_back(r):
        rows_in(other(r + 1)).wait_recv()
        score_in(other(r + 1)).wait_recv()

    loop(E - 1, await_back)
    if E <= 4:
        total = igrecv[0].astype(F32)
        for j in range(1, E):
            total = total + igrecv[j].astype(F32)
    else:
        total = lax.fori_loop(
            0, E, lambda j, t: t + igrecv[j].astype(F32), jnp.zeros((DP * T, rows), F32)
        )
    fsend[...] = total.reshape(DP, T, rows).astype(BF16)
    for p in range(DP):
        hand_on(p).start()

    for k in range(top):
        out = jnp.zeros((T, 128), F32)
        for j in range(E):
            if j % slices == 0:
                per = srecv[j]
                for m in range(1, slices):
                    per = per + srecv[j + m]
                out = out + jnp.where(routes_ref[0, :, k : k + 1] == j // slices, per, 0.0)
        gc_ref[0, :, k : k + 1] = out[:, :1]

    for r in range(1, DP):
        scatter(r).wait_send()

    def sent(i):
        src = source(i)
        for r in range(DP):
            for way in range(2):
                @pl.when(going(src, way))
                def _():
                    relay(src, peer(r), way).wait_send()
        for r in range(1, DP):
            partial_to(src, r).wait_send()

    loop(E, sent)

    def sent_back(r):
        rows_back(other(r + 1)).wait_send()
        score_back(other(r + 1)).wait_send()

    loop(E - 1, sent_back)
    for p in range(DP):
        handed(p).wait_recv()
        passed_ref[0, :, p * rows : (p + 1) * rows] = frecv[p]
    for p in range(DP):
        hand_on(p).wait_send()


def solution(mesh):
    pipes, E, DP = (mesh.shape[a] for a in ("pipe", "expert", "dp"))
    slices = min(8, E // 2)

    def body(tokens, grad_out, routes, combine, w_gate, w_up, w_down):
        T, D = tokens.shape[1:]
        top = routes.shape[2]
        rows, hd = w_gate.shape[1:]
        vmem = pl.BlockSpec(memory_space=pltpu.VMEM)
        hbm = pl.BlockSpec(memory_space=pl.ANY)
        dma = pltpu.SemaphoreType.DMA
        grad = jax.ShapeDtypeStruct((1, rows, hd), F32)
        return pl.pallas_call(
            functools.partial(kernel, (pipes, E, DP, slices)),
            out_shape=(
                jax.ShapeDtypeStruct((1, T, D), BF16),
                jax.ShapeDtypeStruct((1, T, top), F32),
                grad, grad, grad,
            ),
            in_specs=[vmem] * 4 + [hbm] * 3,
            out_specs=[vmem] * 5,
            scratch_shapes=[
                pltpu.VMEM((DP, 2 * T, rows + 128), BF16),
                pltpu.VMEM((E * DP, 2 * T, rows + 128), BF16),
                pltpu.VMEM((rows, 3 * hd), BF16),
                pltpu.VMEM((E * DP, DP * T, 3 * hd), BF16),
                pltpu.VMEM((E * DP, 2 * T, 3 * hd), BF16),
                pltpu.VMEM((E, DP * T, rows), BF16),
                pltpu.VMEM((E, DP * T, rows), BF16),
                pltpu.VMEM((E, DP, T, 128), F32),
                pltpu.VMEM((E, T, 128), F32),
                pltpu.VMEM((DP, T, rows), BF16),
                pltpu.VMEM((DP, T, rows), BF16),
                dma((3,)), dma((DP,)), dma((E, DP)), dma((2, E, DP)),
                dma((E, DP)), dma((E, DP)), dma((E,)), dma((E,)),
                dma((E,)), dma((E,)), dma((DP,)), dma((DP,)),
            ],
            compiler_params=pltpu.CompilerParams(
                collective_id=0, has_side_effects=True, vmem_limit_bytes=48 * 2**20
            ),
        )(tokens, grad_out, routes, combine, w_gate, w_up, w_down)

    weights = P("pipe", "dp", "expert")
    mine = P("pipe", ("expert", "dp"), None)
    return jax.shard_map(
        body, mesh=mesh, in_specs=(mine,) * 4 + (weights,) * 3,
        out_specs=(mine, mine, weights, weights, weights), check_vma=False,
    )
```

time: 135 us -> 43.6 us (0.32)
  Pallas kernels: 0 us -> 33.9 us
  blocking collectives: 31.2 us -> 0 us
  starting transfers between devices: 31.2 us -> 0 us
  waiting for transfers between devices: 29.8 us -> 0 us
  between operations: 14.2 us -> 0.66 us
  matrix products: 8.69 us -> 0 us
  local copies, waits for them, and re-layouts: 14.6 us -> 8.79 us
  other arithmetic: 4.14 us -> 0 us
    pallas_call x0 -> x1, Pallas kernels: none -> 33.9 us  [body(): pl.pallas_call(functools.partial(kernel, (pipes, E, DP, slices)), out_sha...]
    all_gather x3 -> x0, blocking collectives: 31.2 us -> none  [the longest x1 11.6 us: body(): lax.all_gather(w_gate, 'dp', axis=1, tiled=True)]
    all_to_all x5 -> x0, starting transfers between devices: 20.7 us -> none  [the longest x1 5.42 us: body(): lax.all_to_all(replicate_slots(slot_weight), 'expert', split_axis=0, conc...]
    unnamed x2 -> x0, waiting for transfers between devices: 16.4 us -> none
    all_to_all x5 -> x0, waiting for transfers between devices: 13.1 us -> none  [the longest x1 5.52 us: body(): lax.all_to_all(input_rows.reshape(devices, capacity, model_width).astype(...]
    ppermute x1 -> x0, starting transfers between devices: 10.5 us -> none  [from_behind(): return lax.ppermute(block, axis, route)]
    dot_general x14 -> x0, matrix products: 8.69 us -> none  [the longest x1 1.4 us: body(): lax.dot_general(row_inputs, up_grad, contract_first, preferred_element_ty...]
    convert_element_type x5 -> x0, local copies, waits for them, and re-layouts: 2.25 us -> none  [the longest x1 0.77 us: body(): input_rows.reshape(devices, capacity, model_width).astype(jnp.bfloat16)]
  transfers between devices with their start and end apart: 7 -> 0, of which waited for: 5 -> 0; matrix products, arithmetic and copies ran while one was open for 5% -> 0% of each run, Pallas kernels for 0% -> 0%
where the time goes in v1:
time: 43.6 us; the launch traced here: 43.3 us
  Pallas kernels  33.9 us (78%)
  local copies, waits for them, and re-layouts  8.79 us (20%)
  between operations  0.66 us (2%)
    pallas_call x1, Pallas kernels, body(): pl.pallas_call(functools.partial(kernel, (pipes, E, DP, slices)), out_sha...  33.9 us
    unnamed x18, local copies, waits for them, and re-layouts  8.21 us

profile of v1, /device:TPU:1, one launch (start us, length us, event | category | flops | bytes accessed | tf_op | source)
XLA Modules:
  0.0 43.3 jit_solution(10081821176509170172)
XLA Ops:
  0.6 0.0 copy-start.5
  0.6 0.7 %copy.13.comb_ref = bf16[1,8,1]{2,1,0:T(8,128)(2,1)S(1)} copy(bf16[1,8,1]{1,2,0:T(2,128)(2,1)} %param.10) | data formatting | bytes 32 | tf_op args[3]
  1.4 0.0 copy-done.5
  1.4 0.1 copy.12.routes_ref
  1.5 0.0 copy-start
  1.5 0.9 %copy-done = bf16[1,896,128]{2,1,0:T(8,128)(2,1)S(1)} copy-done((bf16[1,896,128]{2,1,0:T(8,128)(2,1)S(1)}, bf16[1,896,128]{2,1,0:T(8,128)(2,1)}, u32[]{:S(2)}) %copy-start) | copy-done | bytes 229400
  2.4 0.0 copy-start.1
  2.4 0.9 %copy-done.1 = bf16[1,896,128]{2,1,0:T(8,128)(2,1)S(1)} copy-done((bf16[1,896,128]{2,1,0:T(8,128)(2,1)S(1)}, bf16[1,896,128]{2,1,0:T(8,128)(2,1)}, u32[]{:S(2)}) %copy-start.1) | copy-done | bytes 229400
  3.4 0.0 copy-start.2
  3.4 0.9 %copy-done.2 = bf16[1,896,128]{2,1,0:T(8,128)(2,1)S(1)} copy-done((bf16[1,896,128]{2,1,0:T(8,128)(2,1)S(1)}, bf16[1,896,128]{2,1,0:T(8,128)(2,1)}, u32[]{:S(2)}) %copy-start.2) | copy-done | bytes 229400
  4.3 0.0 copy-start.3
  4.3 0.8 %copy-done.3 = bf16[1,8,3584]{2,1,0:T(8,128)(2,1)S(1)} copy-done((bf16[1,8,3584]{2,1,0:T(8,128)(2,1)S(1)}, bf16[1,8,3584]{2,1,0:T(8,128)(2,1)}, u32[]{:S(2)}) %copy-start.3) | copy-done | bytes 57368
  5.1 0.0 copy-start.4
  5.1 0.8 %copy-done.4 = bf16[1,8,3584]{2,1,0:T(8,128)(2,1)S(1)} copy-done((bf16[1,8,3584]{2,1,0:T(8,128)(2,1)S(1)}, bf16[1,8,3584]{2,1,0:T(8,128)(2,1)}, u32[]{:S(2)}) %copy-start.4) | copy-done | bytes 57368
  5.9 33.9 %shard_map.110 = (bf16[1,8,3584]{2,1,0:T(8,128)(2,1)S(1)}, f32[1,8,1]{2,1,0:T(8,128)S(1)}, f32[1,896,128]{2,1,0:T(8,128)S(1)}, f32[1,896,128]{2,1,0:T(8,128)S(1)}, f32[1,896,128]{2,1,0:T(8,128)S(1)}) custom-call(bf16[1,8,3584]{2,1,0:T(8,128)(2,1)S(1)} %copy-done.3, bf16[1,8,3584]{2,1,0:T(8,128)(2,1)S(1)} %copy-done.4, s32[1,8,1]{2,1,0:T(8,128)S(1)} %copy.12.routes_ref, ...), custom_call_target="tpu_custom_call" | custom-call | tf_op jit(solution)/shard_map/pallas_call | solution.py:300
  39.8 0.6 %copy.14 = f32[1,8,1]{1,2,0:T(1,128)} copy(f32[1,8,1]{2,1,0:T(8,128)S(1)} %get-tuple-element.6) | data formatting | bytes 64 | tf_op jit(solution)/shard_map/pallas_call | solution.py:300
  40.4 0.6 %copy.19 = bf16[1,8,3584]{2,1,0:T(8,128)(2,1)} copy(bf16[1,8,3584]{2,1,0:T(8,128)(2,1)S(1)} %get-tuple-element.15) | data formatting | bytes 114688
  41.0 0.8 %copy.20 = f32[1,896,128]{2,1,0:T(8,128)} copy(f32[1,896,128]{2,1,0:T(8,128)S(1)} %get-tuple-element.17) | data formatting | bytes 917504
  41.8 0.8 %copy.21 = f32[1,896,128]{2,1,0:T(8,128)} copy(f32[1,896,128]{2,1,0:T(8,128)S(1)} %get-tuple-element.18) | data formatting | bytes 917504
  42.5 0.8 %copy.22 = f32[1,896,128]{2,1,0:T(8,128)} copy(f32[1,896,128]{2,1,0:T(8,128)S(1)} %get-tuple-element.19) | data formatting | bytes 917504
Async XLA Ops:
  0.6 0.8 %copy-start.5 = (s32[1,8,1]{1,2,0:T(1,128)S(1)}, s32[1,8,1]{1,2,0:T(1,128)}, u32[]{:S(2)}) copy-start(s32[1,8,1]{1,2,0:T(1,128)} %param.9) | copy-start | bytes 100
  1.5 0.9 %copy-start = (bf16[1,896,128]{2,1,0:T(8,128)(2,1)S(1)}, bf16[1,896,128]{2,1,0:T(8,128)(2,1)}, u32[]{:S(2)}) copy-start(bf16[1,896,128]{2,1,0:T(8,128)(2,1)} %wg_hbm.1) | copy-start | bytes 688132
  2.4 0.9 %copy-start.1 = (bf16[1,896,128]{2,1,0:T(8,128)(2,1)S(1)}, bf16[1,896,128]{2,1,0:T(8,128)(2,1)}, u32[]{:S(2)}) copy-start(bf16[1,896,128]{2,1,0:T(8,128)(2,1)} %wu_hbm.1) | copy-start | bytes 688132
  3.4 0.9 %copy-start.2 = (bf16[1,896,128]{2,1,0:T(8,128)(2,1)S(1)}, bf16[1,896,128]{2,1,0:T(8,128)(2,1)}, u32[]{:S(2)}) copy-start(bf16[1,896,128]{2,1,0:T(8,128)(2,1)} %wd_hbm.1) | copy-start | bytes 688132
  4.3 0.8 %copy-start.3 = (bf16[1,8,3584]{2,1,0:T(8,128)(2,1)S(1)}, bf16[1,8,3584]{2,1,0:T(8,128)(2,1)}, u32[]{:S(2)}) copy-start(bf16[1,8,3584]{2,1,0:T(8,128)(2,1)} %tok_ref.1) | copy-start | bytes 172036
  5.1 0.8 %copy-start.4 = (bf16[1,8,3584]{2,1,0:T(8,128)(2,1)S(1)}, bf16[1,8,3584]{2,1,0:T(8,128)(2,1)}, u32[]{:S(2)}) copy-start(bf16[1,8,3584]{2,1,0:T(8,128)(2,1)} %go_ref.1) | copy-start | bytes 172036

commit v2 on v1

--- a/solution.py
+++ b/solution.py
@@ -22,14 +22,18 @@
 
 
 def kernel(
-    sizes, tok_ref, go_ref, routes_ref, comb_ref, wg_hbm, wu_hbm, wd_hbm,
-    passed_ref, gc_ref, gg_ref, gu_ref, gd_ref,
-    stage, xg, wcat, qbuf, hbuf, igsend, igrecv, ssend, srecv, fsend, frecv,
-    wsem, p1s, gr, zs, qs, qr, igs, igr, ss, sr, fs, fr,
+    sizes, tok_hbm, go_hbm, routes_hbm, comb_hbm, wg_hbm, wu_hbm, wd_hbm,
+    *rest,
 ):
+    outs, rest = rest[:5], rest[5:]
+    passed_ref, gc_ref, gg_ref, gu_ref, gd_ref, osem = rest[:6]
+    (
+    tok_ref, go_ref, routes_ref, comb_ref, stage, xg, wcat, qbuf, hbuf, igsend, igrecv, ssend, srecv, fsend, frecv,
+    isem, wsem, p1s, gr, zs, qs, qr, igs, igr, ss, sr, fs, fr,
+    ) = rest[6:]
     pipes, E, DP, slices = sizes
     T = tok_ref.shape[1]
-    top = routes_ref.shape[2]
+    top = routes_ref.shape[1]
     rows, hd = wg_hbm.shape[1:]
     pipe, e, d = (lax.axis_index(a) for a in ("pipe", "expert", "dp"))
     behind = lax.rem(pipe + pipes - 1, pipes)
@@ -51,6 +55,17 @@
     loop(E - 1, lambda r: greet(pipe, other(r + 1), d))
     loop(DP, lambda r: greet(ahead, e, r))
 
+    given = [
+        pltpu.make_async_copy(a, b, isem.at[i])
+        for i, (a, b) in enumerate(
+            (
+                (routes_hbm, routes_ref), (comb_hbm, comb_ref),
+                (tok_hbm, tok_ref), (go_hbm, go_ref),
+            )
+        )
+    ]
+    for c in given:
+        c.start()
     loads = [
         pltpu.make_async_copy(w.at[0], wcat.at[:, pl.ds(i * hd, hd)], wsem.at[i])
         for i, w in enumerate((wg_hbm, wu_hbm, wd_hbm))
@@ -59,11 +74,21 @@
         c.start()
 
     lane = lax.broadcasted_iota(jnp.int32, (T, 128), 1)
+    diagonal = lane == lax.broadcasted_iota(jnp.int32, (T, 128), 0)
+    for c in given[:2]:
+        c.wait()
+
+    def column(row):
+        spread = jnp.broadcast_to(row, (T, T))
+        return jnp.sum(jnp.where(diagonal[:, :T], spread, 0), axis=1, keepdims=True)
+
+    named = [column(routes_ref[0, k : k + 1, :]) for k in range(top)]
     weight = jnp.zeros((T, 128), F32)
     for k in range(top):
-        weight = weight + jnp.where(
-            routes_ref[0, :, k : k + 1] == lane, comb_ref[0, :, k : k + 1].astype(F32), 0.0
-        )
+        share = column(comb_ref[0, k : k + 1, :].astype(F32))
+        weight = weight + jnp.where(named[k] == lane, share, 0.0)
+    for c in given[2:]:
+        c.wait()
     tail = jnp.concatenate([weight, jnp.zeros_like(weight)], axis=0).astype(BF16)
     for p in range(DP):
         both = jnp.concatenate(
@@ -231,6 +256,13 @@
             for i, ref in enumerate((gg_ref, gu_ref, gd_ref)):
                 ref[0] = ref[0] + grads[:, i * hd : (i + 1) * hd]
 
+    results = [
+        pltpu.make_async_copy(a, b, osem.at[i])
+        for i, (a, b) in enumerate(zip((passed_ref, gc_ref, gg_ref, gu_ref, gd_ref), outs))
+    ]
+    for c in results[2:]:
+        c.start()
+
     def await_back(r):
         rows_in(other(r + 1)).wait_recv()
         score_in(other(r + 1)).wait_recv()
@@ -255,8 +287,10 @@
                 per = srecv[j]
                 for m in range(1, slices):
                     per = per + srecv[j + m]
-                out = out + jnp.where(routes_ref[0, :, k : k + 1] == j // slices, per, 0.0)
-        gc_ref[0, :, k : k + 1] = out[:, :1]
+                out = out + jnp.where(named[k] == j // slices, per, 0.0)
+        row = jnp.sum(jnp.where(diagonal, out, 0.0), axis=0, keepdims=True)
+        gc_ref[0, k : k + 1, :] = row[:, :T]
+    results[1].start()
 
     for r in range(1, DP):
         scatter(r).wait_send()
@@ -281,8 +315,23 @@
     for p in range(DP):
         handed(p).wait_recv()
         passed_ref[0, :, p * rows : (p + 1) * rows] = frecv[p]
+    results[0].start()
     for p in range(DP):
         hand_on(p).wait_send()
+    for c in results:
+        c.wait()
+
+
+def write_out(*refs):
+    count = len(refs) // 2
+    sems = refs[-1]
+    copies = [
+        pltpu.make_async_copy(refs[i], refs[count + i], sems.at[i]) for i in range(count)
+    ]
+    for c in copies:
+        c.start()
+    for c in copies:
+        c.wait()
 
 
 def solution(mesh):
@@ -293,20 +342,25 @@
         T, D = tokens.shape[1:]
         top = routes.shape[2]
         rows, hd = w_gate.shape[1:]
-        vmem = pl.BlockSpec(memory_space=pltpu.VMEM)
-        hbm = pl.BlockSpec(memory_space=pl.ANY)
+        hbm = pl.BlockSpec(memory_space=pltpu.HBM)
         dma = pltpu.SemaphoreType.DMA
         grad = jax.ShapeDtypeStruct((1, rows, hd), F32)
-        return pl.pallas_call(
+        shapes = (
+            jax.ShapeDtypeStruct((1, T, D), BF16),
+            jax.ShapeDtypeStruct((1, top, T), F32),
+            grad, grad, grad,
+        )
+        results = pl.pallas_call(
             functools.partial(kernel, (pipes, E, DP, slices)),
-            out_shape=(
-                jax.ShapeDtypeStruct((1, T, D), BF16),
-                jax.ShapeDtypeStruct((1, T, top), F32),
-                grad, grad, grad,
-            ),
-            in_specs=[vmem] * 4 + [hbm] * 3,
-            out_specs=[vmem] * 5,
+            out_shape=shapes,
+            in_specs=[hbm] * 7,
+            out_specs=[hbm] * 5,
             scratch_shapes=[
+                *(pltpu.VMEM(a.shape, a.dtype) for a in shapes), dma((5,)),
+                pltpu.VMEM((1, T, D), BF16),
+                pltpu.VMEM((1, T, D), BF16),
+                pltpu.VMEM((1, top, T), jnp.int32),
+                pltpu.VMEM((1, top, T), BF16),
                 pltpu.VMEM((DP, 2 * T, rows + 128), BF16),
                 pltpu.VMEM((E * DP, 2 * T, rows + 128), BF16),
                 pltpu.VMEM((rows, 3 * hd), BF16),
@@ -318,14 +372,26 @@
                 pltpu.VMEM((E, T, 128), F32),
                 pltpu.VMEM((DP, T, rows), BF16),
                 pltpu.VMEM((DP, T, rows), BF16),
-                dma((3,)), dma((DP,)), dma((E, DP)), dma((2, E, DP)),
+                dma((4,)), dma((3,)), dma((DP,)), dma((E, DP)), dma((2, E, DP)),
                 dma((E, DP)), dma((E, DP)), dma((E,)), dma((E,)),
                 dma((E,)), dma((E,)), dma((DP,)), dma((DP,)),
             ],
             compiler_params=pltpu.CompilerParams(
-                collective_id=0, has_side_effects=True, vmem_limit_bytes=48 * 2**20
+                collective_id=0, has_side_effects=True, vmem_limit_bytes=64 * 2**20
             ),
-        )(tokens, grad_out, routes, combine, w_gate, w_up, w_down)
+        )(
+            tokens, grad_out, jnp.swapaxes(routes, 1, 2), jnp.swapaxes(combine, 1, 2),
+            w_gate, w_up, w_down,
+        )
+        passed, grad_combine, *grads = pl.pallas_call(
+            write_out,
+            out_shape=shapes,
+            in_specs=[hbm] * 5,
+            out_specs=[hbm] * 5,
+            scratch_shapes=[dma((5,))],
+            compiler_params=pltpu.CompilerParams(vmem_limit_bytes=64 * 2**20),
+        )(*results)
+        return (passed, jnp.swapaxes(grad_combine, 1, 2), *grads)
 
     weights = P("pipe", "dp", "expert")
     mine = P("pipe", ("expert", "dp"), None)

time: 43.6 us -> 80 us (1.83)
  Pallas kernels: 33.9 us -> 79.2 us
  local copies, waits for them, and re-layouts: 8.79 us -> 0 us
    pallas_call x0 -> x1, Pallas kernels: none -> 44.6 us  [body(): pl.pallas_call(write_out, out_shape=shapes, in_specs=[hbm] * 5, out_specs...]
    unnamed x18 -> x0, local copies, waits for them, and re-layouts: 8.21 us -> none
where the time goes in v2:
time: 80 us; the launch traced here: 79.9 us
  Pallas kernels  79.2 us (99%)
    pallas_call x1, Pallas kernels, body(): pl.pallas_call(write_out, out_shape=shapes, in_specs=[hbm] * 5, out_specs...  44.6 us
    pallas_call x1, Pallas kernels, body(): pl.pallas_call(functools.partial(kernel, (pipes, E, DP, slices)), out_sha...  34.6 us

profile of v2, /device:TPU:1, one launch (start us, length us, event | category | flops | bytes accessed | tf_op | source)
XLA Modules:
  0.0 79.9 jit_solution(4159093461972034581)
XLA Ops:
  0.6 34.6 %shard_map.110 = (bf16[1,8,3584]{2,1,0:T(8,128)(2,1)}, f32[1,1,8]{2,1,0:T(1,128)}, f32[1,896,128]{2,1,0:T(8,128)}, f32[1,896,128]{2,1,0:T(8,128)}, f32[1,896,128]{2,1,0:T(8,128)}) custom-call(bf16[1,8,3584]{2,1,0:T(8,128)(2,1)} %tok_hbm.1, bf16[1,8,3584]{2,1,0:T(8,128)(2,1)} %go_hbm.1, s32[1,1,8]{2,1,0:T(1,128)} %bitcast.3, bf16[1,1,8]{2,1,0:T(2,128)(2,1)} %bitcast.4, ...), custom_call_target="tpu_custom_call" | custom-call | tf_op jit(solution)/shard_map/pallas_call | solution.py:353
  35.3 44.6 %shard_map.111 = (bf16[1,8,3584]{2,1,0:T(8,128)(2,1)}, f32[1,1,8]{2,1,0:T(1,128)}, f32[1,896,128]{2,1,0:T(8,128)}, f32[1,896,128]{2,1,0:T(8,128)}, f32[1,896,128]{2,1,0:T(8,128)}) custom-call(bf16[1,8,3584]{2,1,0:T(8,128)(2,1)} %get-tuple-element.15.refs_0_, f32[1,1,8]{2,1,0:T(1,128)} %get-tuple-element.16.refs_1_, ...), custom_call_target="tpu_custom_call" | custom-call | tf_op jit(solution)/shard_map/pallas_call | solution.py:386

commit v3 on v2

--- a/solution.py
+++ b/solution.py
@@ -23,14 +23,10 @@
 
 def kernel(
     sizes, tok_hbm, go_hbm, routes_hbm, comb_hbm, wg_hbm, wu_hbm, wd_hbm,
-    *rest,
-):
-    outs, rest = rest[:5], rest[5:]
-    passed_ref, gc_ref, gg_ref, gu_ref, gd_ref, osem = rest[:6]
-    (
+    passed_ref, gc_ref, gg_ref, gu_ref, gd_ref,
     tok_ref, go_ref, routes_ref, comb_ref, stage, xg, wcat, qbuf, hbuf, igsend, igrecv, ssend, srecv, fsend, frecv,
     isem, wsem, p1s, gr, zs, qs, qr, igs, igr, ss, sr, fs, fr,
-    ) = rest[6:]
+):
     pipes, E, DP, slices = sizes
     T = tok_ref.shape[1]
     top = routes_ref.shape[1]
@@ -256,13 +252,6 @@
             for i, ref in enumerate((gg_ref, gu_ref, gd_ref)):
                 ref[0] = ref[0] + grads[:, i * hd : (i + 1) * hd]
 
-    results = [
-        pltpu.make_async_copy(a, b, osem.at[i])
-        for i, (a, b) in enumerate(zip((passed_ref, gc_ref, gg_ref, gu_ref, gd_ref), outs))
-    ]
-    for c in results[2:]:
-        c.start()
-
     def await_back(r):
         rows_in(other(r + 1)).wait_recv()
         score_in(other(r + 1)).wait_recv()
@@ -290,7 +279,6 @@
                 out = out + jnp.where(named[k] == j // slices, per, 0.0)
         row = jnp.sum(jnp.where(diagonal, out, 0.0), axis=0, keepdims=True)
         gc_ref[0, k : k + 1, :] = row[:, :T]
-    results[1].start()
 
     for r in range(1, DP):
         scatter(r).wait_send()
@@ -315,11 +303,8 @@
     for p in range(DP):
         handed(p).wait_recv()
         passed_ref[0, :, p * rows : (p + 1) * rows] = frecv[p]
-    results[0].start()
     for p in range(DP):
         hand_on(p).wait_send()
-    for c in results:
-        c.wait()
 
 
 def write_out(*refs):
@@ -342,6 +327,7 @@
         T, D = tokens.shape[1:]
         top = routes.shape[2]
         rows, hd = w_gate.shape[1:]
+        vmem = pl.BlockSpec(memory_space=pltpu.VMEM)
         hbm = pl.BlockSpec(memory_space=pltpu.HBM)
         dma = pltpu.SemaphoreType.DMA
         grad = jax.ShapeDtypeStruct((1, rows, hd), F32)
@@ -354,9 +340,8 @@
             functools.partial(kernel, (pipes, E, DP, slices)),
             out_shape=shapes,
             in_specs=[hbm] * 7,
-            out_specs=[hbm] * 5,
+            out_specs=[vmem] * 5,
             scratch_shapes=[
-                *(pltpu.VMEM(a.shape, a.dtype) for a in shapes), dma((5,)),
                 pltpu.VMEM((1, T, D), BF16),
                 pltpu.VMEM((1, T, D), BF16),
                 pltpu.VMEM((1, top, T), jnp.int32),
@@ -377,19 +362,23 @@
                 dma((E,)), dma((E,)), dma((DP,)), dma((DP,)),
             ],
             compiler_params=pltpu.CompilerParams(
-                collective_id=0, has_side_effects=True, vmem_limit_bytes=64 * 2**20
+                collective_id=0, has_side_effects=True, vmem_limit_bytes=48 * 2**20
             ),
         )(
-            tokens, grad_out, jnp.swapaxes(routes, 1, 2), jnp.swapaxes(combine, 1, 2),
-            w_gate, w_up, w_down,
+            *(
+                pltpu.with_memory_space_constraint(a, pltpu.HBM)
+                for a in (
+                    tokens, grad_out, jnp.swapaxes(routes, 1, 2), jnp.swapaxes(combine, 1, 2),
+                    w_gate, w_up, w_down,
+                )
+            )
         )
         passed, grad_combine, *grads = pl.pallas_call(
             write_out,
             out_shape=shapes,
-            in_specs=[hbm] * 5,
+            in_specs=[vmem] * 5,
             out_specs=[hbm] * 5,
             scratch_shapes=[dma((5,))],
-            compiler_params=pltpu.CompilerParams(vmem_limit_bytes=64 * 2**20),
         )(*results)
         return (passed, jnp.swapaxes(grad_combine, 1, 2), *grads)
 

time: 80 us -> 40.7 us (0.51)
  Pallas kernels: 79.2 us -> 36.4 us
  local copies, waits for them, and re-layouts: 0 us -> 3.47 us
    pallas_call x1, Pallas kernels: 44.6 us -> 2.46 us  [body(): pl.pallas_call(write_out, out_shape=shapes, in_specs=[vmem] * 5, out_spec...]
    unnamed x0 -> x10, local copies, waits for them, and re-layouts: none -> 3.47 us
where the time goes in v3:
time: 40.7 us; the launch traced here: 40.5 us
  Pallas kernels  36.4 us (89%)
  local copies, waits for them, and re-layouts  3.47 us (9%)
  between operations  0.65 us (2%)
    pallas_call x1, Pallas kernels, body(): pl.pallas_call(functools.partial(kernel, (pipes, E, DP, slices)), out_sha...  34 us
    unnamed x10, local copies, waits for them, and re-layouts  3.47 us
    pallas_call x1, Pallas kernels, body(): pl.pallas_call(write_out, out_shape=shapes, in_specs=[vmem] * 5, out_spec...  2.46 us

profile of v3, /device:TPU:1, one launch (start us, length us, event | category | flops | bytes accessed | tf_op | source)
XLA Modules:
  0.0 40.5 jit_solution(3827294577034474288)
XLA Ops:
  0.6 34.0 %shard_map.110 = (bf16[1,8,3584]{2,1,0:T(8,128)(2,1)S(1)}, f32[1,1,8]{2,1,0:T(1,128)S(1)}, f32[1,896,128]{2,1,0:T(8,128)S(1)}, f32[1,896,128]{2,1,0:T(8,128)S(1)}, f32[1,896,128]{2,1,0:T(8,128)S(1)}) custom-call(bf16[1,8,3584]{2,1,0:T(8,128)(2,1)} %tok_hbm.1, bf16[1,8,3584]{2,1,0:T(8,128)(2,1)} %go_hbm.1, s32[1,1,8]{2,1,0:T(1,128)} %bitcast.3, ...), custom_call_target="tpu_custom_call" | custom-call | tf_op jit(solution)/shard_map/pallas_call | solution.py:339
  34.6 0.0 copy-start
  34.6 0.8 %copy-done = f32[1,896,128]{2,1,0:T(8,128)} copy-done((f32[1,896,128]{2,1,0:T(8,128)}, f32[1,896,128]{2,1,0:T(8,128)S(1)}, u32[]{:S(2)}) %copy-start) | copy-done | bytes 458776
  35.4 0.0 copy-start.1
  35.4 0.8 %copy-done.1 = f32[1,896,128]{2,1,0:T(8,128)} copy-done((f32[1,896,128]{2,1,0:T(8,128)}, f32[1,896,128]{2,1,0:T(8,128)S(1)}, u32[]{:S(2)}) %copy-start.1) | copy-done | bytes 458776
  36.2 0.0 copy-start.2
  36.2 0.8 %copy-done.2 = f32[1,896,128]{2,1,0:T(8,128)} copy-done((f32[1,896,128]{2,1,0:T(8,128)}, f32[1,896,128]{2,1,0:T(8,128)S(1)}, u32[]{:S(2)}) %copy-start.2) | copy-done | bytes 458776
  36.9 0.0 copy-start.3
  36.9 0.6 %copy-done.3 = bf16[1,8,3584]{2,1,0:T(8,128)(2,1)} copy-done((bf16[1,8,3584]{2,1,0:T(8,128)(2,1)}, bf16[1,8,3584]{2,1,0:T(8,128)(2,1)S(1)}, u32[]{:S(2)}) %copy-start.3) | copy-done | bytes 57368
  37.6 0.0 copy-start.4
  37.6 0.5 %copy-done.4 = f32[1,1,8]{2,1,0:T(1,128)} copy-done((f32[1,1,8]{2,1,0:T(1,128)}, f32[1,1,8]{2,1,0:T(1,128)S(1)}, u32[]{:S(2)}) %copy-start.4) | copy-done | bytes 56
  38.1 2.5 %shard_map.111 = (bf16[1,8,3584]{2,1,0:T(8,128)(2,1)}, f32[1,1,8]{2,1,0:T(1,128)}, f32[1,896,128]{2,1,0:T(8,128)}, f32[1,896,128]{2,1,0:T(8,128)}, f32[1,896,128]{2,1,0:T(8,128)}) custom-call(bf16[1,8,3584]{2,1,0:T(8,128)(2,1)} %copy-done.3, f32[1,1,8]{2,1,0:T(1,128)} %copy-done.4, f32[1,896,128]{2,1,0:T(8,128)} %copy-done, f32[1,896,128]{2,1,0:T(8,128)} %copy-done.1, ...), custom_call_target="tpu_custom_call" | custom-call | tf_op jit(solution)/shard_map/pallas_call | solution.py:376
Async XLA Ops:
  34.6 0.8 %copy-start = (f32[1,896,128]{2,1,0:T(8,128)}, f32[1,896,128]{2,1,0:T(8,128)S(1)}, u32[]{:S(2)}) copy-start(f32[1,896,128]{2,1,0:T(8,128)S(1)} %get-tuple-element.17.refs_2_) | copy-start | bytes 1376260
  35.4 0.8 %copy-start.1 = (f32[1,896,128]{2,1,0:T(8,128)}, f32[1,896,128]{2,1,0:T(8,128)S(1)}, u32[]{:S(2)}) copy-start(f32[1,896,128]{2,1,0:T(8,128)S(1)} %get-tuple-element.18.refs_3_) | copy-start | bytes 1376260
  36.2 0.8 %copy-start.2 = (f32[1,896,128]{2,1,0:T(8,128)}, f32[1,896,128]{2,1,0:T(8,128)S(1)}, u32[]{:S(2)}) copy-start(f32[1,896,128]{2,1,0:T(8,128)S(1)} %get-tuple-element.19.refs_4_) | copy-start | bytes 1376260
  36.9 0.6 %copy-start.3 = (bf16[1,8,3584]{2,1,0:T(8,128)(2,1)}, bf16[1,8,3584]{2,1,0:T(8,128)(2,1)S(1)}, u32[]{:S(2)}) copy-start(bf16[1,8,3584]{2,1,0:T(8,128)(2,1)S(1)} %get-tuple-element.15.refs_0_) | copy-start | bytes 172036
  37.6 0.5 %copy-start.4 = (f32[1,1,8]{2,1,0:T(1,128)}, f32[1,1,8]{2,1,0:T(1,128)S(1)}, u32[]{:S(2)}) copy-start(f32[1,1,8]{2,1,0:T(1,128)S(1)} %get-tuple-element.16.refs_1_) | copy-start | bytes 100

commit v4 on v3

--- a/solution.py
+++ b/solution.py
@@ -379,6 +379,7 @@
             in_specs=[vmem] * 5,
             out_specs=[hbm] * 5,
             scratch_shapes=[dma((5,))],
+            compiler_params=pltpu.CompilerParams(vmem_limit_bytes=2 * 2**20),
         )(*results)
         return (passed, jnp.swapaxes(grad_combine, 1, 2), *grads)
 

time: 40.7 us -> 35.9 us (0.88)
  local copies, waits for them, and re-layouts: 3.47 us -> 0 us
  Pallas kernels: 36.4 us -> 35.1 us
    unnamed x10 -> x0, local copies, waits for them, and re-layouts: 3.47 us -> none
    pallas_call x1, Pallas kernels: 2.46 us -> 1.14 us  [body(): pl.pallas_call(write_out, out_shape=shapes, in_specs=[vmem] * 5, out_spec...]
where the time goes in v4:
time: 35.9 us; the launch traced here: 35.7 us
  Pallas kernels  35.1 us (98%)
  between operations  0.64 us (2%)
    pallas_call x1, Pallas kernels, body(): pl.pallas_call(functools.partial(kernel, (pipes, E, DP, slices)), out_sha...  34 us
    pallas_call x1, Pallas kernels, body(): pl.pallas_call(write_out, out_shape=shapes, in_specs=[vmem] * 5, out_spec...  1.14 us

profile of v4, /device:TPU:1, one launch (start us, length us, event | category | flops | bytes accessed | tf_op | source)
XLA Modules:
  0.0 35.7 jit_solution(1010954413908532906)
XLA Ops:
  0.6 34.0 %shard_map.110 = (bf16[1,8,3584]{2,1,0:T(8,128)(2,1)S(1)}, f32[1,1,8]{2,1,0:T(1,128)S(1)}, f32[1,896,128]{2,1,0:T(8,128)S(1)}, f32[1,896,128]{2,1,0:T(8,128)S(1)}, f32[1,896,128]{2,1,0:T(8,128)S(1)}) custom-call(bf16[1,8,3584]{2,1,0:T(8,128)(2,1)} %tok_hbm.1, bf16[1,8,3584]{2,1,0:T(8,128)(2,1)} %go_hbm.1, s32[1,1,8]{2,1,0:T(1,128)} %bitcast.3, ...), custom_call_target="tpu_custom_call" | custom-call | tf_op jit(solution)/shard_map/pallas_call | solution.py:339
  34.6 1.1 %shard_map.111 = (bf16[1,8,3584]{2,1,0:T(8,128)(2,1)}, f32[1,1,8]{2,1,0:T(1,128)}, f32[1,896,128]{2,1,0:T(8,128)}, f32[1,896,128]{2,1,0:T(8,128)}, f32[1,896,128]{2,1,0:T(8,128)}) custom-call(bf16[1,8,3584]{2,1,0:T(8,128)(2,1)S(1)} %get-tuple-element.15.refs_0_, f32[1,1,8]{2,1,0:T(1,128)S(1)} %get-tuple-element.16.refs_1_, ...), custom_call_target="tpu_custom_call" | custom-call | tf_op jit(solution)/shard_map/pallas_call | solution.py:376

commit v5 on v4

--- a/solution.py
+++ b/solution.py
@@ -24,8 +24,9 @@
 def kernel(
     sizes, tok_hbm, go_hbm, routes_hbm, comb_hbm, wg_hbm, wu_hbm, wd_hbm,
     passed_ref, gc_ref, gg_ref, gu_ref, gd_ref,
-    tok_ref, go_ref, routes_ref, comb_ref, stage, xg, wcat, qbuf, hbuf, igsend, igrecv, ssend, srecv, fsend, frecv,
-    isem, wsem, p1s, gr, zs, qs, qr, igs, igr, ss, sr, fs, fr,
+    tok_ref, go_ref, routes_ref, comb_ref, stage, xg, wcat, packed, away, shares, shares_away,
+    qbuf, hbuf, igsend, igrecv, ssend, srecv, fsend, frecv,
+    isem, wsem, p1s, p1r, aws, gr, zs, qs, qr, igs, igr, ss, sr, fs, fr,
 ):
     pipes, E, DP, slices = sizes
     T = tok_ref.shape[1]
@@ -35,6 +36,12 @@
     behind = lax.rem(pipe + pipes - 1, pipes)
     ahead = lax.rem(pipe + 1, pipes)
     my_expert = e // slices
+    first, last_one = my_expert * slices, my_expert * slices + slices - 1
+    experts = E // slices
+    cap = min(T, max(2, 3 * T * top // (2 * experts)))
+    slots = DP * cap
+    pieces = 2 * slots // 16
+    padded = DP * T
 
     def peer(r):
         return lax.rem(d + r, DP)
@@ -85,7 +92,7 @@
         weight = weight + jnp.where(named[k] == lane, share, 0.0)
     for c in given[2:]:
         c.wait()
-    tail = jnp.concatenate([weight, jnp.zeros_like(weight)], axis=0).astype(BF16)
+    tail = jnp.concatenate([weight, weight], axis=0).astype(BF16)
     for p in range(DP):
         both = jnp.concatenate(
             [
@@ -107,17 +114,29 @@
 
     def scatter(r):
         to = peer(r)
-        return remote(stage.at[to], xg.at[e * DP + d], p1s.at[r], gr.at[e, d], (pipe, e, to))
+        return remote(stage.at[to], xg.at[d], p1s.at[r], p1r.at[d], (pipe, e, to))
+
+    def scattered(r):
+        p = peer(r)
+        return remote(stage.at[p], xg.at[p], p1s.at[r], p1r.at[p], (pipe, e, p))
+
+    def part(src, p):
+        return shares.at[src] if p == pieces else packed.at[src, p]
+
+    def send_away(j, p):
+        to = jnp.where(j > my_expert, j * slices, j * slices + slices - 1)
+        block = shares_away.at[j] if p == pieces else away.at[j, p]
+        return remote(block, part(e, p), aws.at[j, p], gr.at[e, p], (pipe, to, d))
 
     def relay(src, p, way):
-        block = xg.at[src * DP + p]
+        block = part(src, p)
         to = jnp.clip(e + (1 if way == 0 else -1), 0, E - 1)
         return remote(block, block, zs.at[way, src, p], gr.at[src, p], (pipe, to, d))
 
     def going(src, way):
         if way == 0:
-            return jnp.logical_and(src <= e, e + 1 < E)
-        return jnp.logical_and(src >= e, e > 0)
+            return jnp.logical_and(src <= e, e < last_one)
+        return jnp.logical_and(src >= e, e > first)
 
     def partial_to(src, r):
         block = qbuf.at[src * DP + d]
@@ -132,13 +151,13 @@
         return remote(igsend.at[src], igrecv.at[e], igs.at[src], igr.at[e], (pipe, src, d))
 
     def score_back(src):
-        return remote(ssend.at[src, d], srecv.at[e], ss.at[src], sr.at[e], (pipe, src, d))
+        return remote(ssend.at[src], srecv.at[e], ss.at[src], sr.at[e], (pipe, src, d))
 
     def rows_in(src):
         return remote(igsend.at[src], igrecv.at[src], igs.at[src], igr.at[src], (pipe, src, d))
 
     def score_in(src):
-        return remote(ssend.at[src, d], srecv.at[src], ss.at[src], sr.at[src], (pipe, src, d))
+        return remote(ssend.at[src], srecv.at[src], ss.at[src], sr.at[src], (pipe, src, d))
 
     def hand_on(p):
         return remote(fsend.at[p], frecv.at[d], fs.at[p], fr.at[d], (behind, e, p))
@@ -148,7 +167,42 @@
 
     for r in range(1, DP):
         scatter(r).start()
-    xg[e * DP + d] = stage[d]
+    xg[d] = stage[d]
+
+    count = DP * 2 * T
+    at_row = lax.broadcasted_iota(jnp.int32, (count, 128), 0)
+    at_lane = lax.broadcasted_iota(jnp.int32, (count, 128), 1)
+    square_row = lax.broadcasted_iota(jnp.int32, (count, count), 0)
+    square_col = lax.broadcasted_iota(jnp.int32, (count, count), 1)
+    earlier = jnp.logical_and(square_row // T == square_col // T, square_col < square_row)
+    base = (at_row // (2 * T)) * cap + (at_row // T) % 2 * slots
+    for r in range(1, DP):
+        scattered(r).wait_recv()
+    plane = xg[...].reshape(count, rows + 128)
+    plane_weight = plane[:, rows:].astype(F32)
+    plane_rows = plane[:, :rows]
+    here = jnp.where(plane_weight > 0.0, 1.0, 0.0)
+    rank = jnp.dot(
+        jnp.where(earlier, 1.0, 0.0).astype(BF16), here.astype(BF16), preferred_element_type=F32
+    )
+    slot = jnp.where(here > 0.0, base.astype(F32) + rank, -1.0)
+
+    def pack(j):
+        mine = at_lane == j
+        to = jnp.sum(jnp.where(mine, slot, 0.0), axis=1, keepdims=True)
+        share = jnp.sum(jnp.where(mine, plane_weight, 0.0), axis=1, keepdims=True)
+        chosen = at_lane.astype(F32) == to
+        row = jnp.sum(jnp.where(chosen, share, 0.0), axis=0, keepdims=True)
+        onehot = jnp.where(chosen, 1.0, 0.0)[:, : 2 * slots].astype(BF16)
+        moved = lax.dot_general(onehot, plane_rows, contract_first, preferred_element_type=F32)
+        return moved.astype(BF16).reshape(pieces, 16, rows), jnp.broadcast_to(row, (8, 128))
+
+    for k in range(1, experts):
+        j = lax.rem(my_expert + k, experts)
+        away[j], shares_away[j] = pack(j)
+        for p in range(pieces + 1):
+            send_away(j, p).start()
+    packed[e], shares[e] = pack(my_expert)
 
     near = jnp.minimum(e, E - 1 - e)
 
@@ -159,11 +213,10 @@
         one_side = jnp.where(e < E - 1 - e, e + (i - near), e - (i - near))
         return jnp.where(i <= 2 * near, both_sides, one_side)
 
-    def arrive(i, first):
-        src = e if first else source(i)
-        for r in range(DP):
-            p = peer(r)
-            if not (first and r == 0):
+    def arrive(i, own):
+        src = e if own else source(i)
+        for p in range(pieces + 1):
+            if not own:
                 relay(src, p, 0).wait_recv()
             for way in range(2):
                 @pl.when(going(src, way))
@@ -172,11 +225,11 @@
         return src
 
     def project(src):
-        block = xg[pl.ds(src * DP, DP)][:, :, :rows].reshape(DP * 2 * T, rows)
-        part = jnp.dot(block, wcat[...], preferred_element_type=F32)
-        part = part.reshape(DP, 2 * T, 3 * hd)
-        q = jnp.concatenate([part[:, :T, : 2 * hd], part[:, T:, 2 * hd :]], axis=2)
-        qbuf[src * DP + d] = q.reshape(DP * T, 3 * hd).astype(BF16)
+        block = packed[src].reshape(2 * slots, rows)
+        sums = jnp.dot(block, wcat[...], preferred_element_type=F32)
+        q = jnp.concatenate([sums[:slots, : 2 * hd], sums[slots:, 2 * hd :]], axis=1)
+        filler = jnp.zeros((padded - slots, 3 * hd), F32)
+        qbuf[src * DP + d] = jnp.concatenate([q, filler], axis=0).astype(BF16)
         for r in range(1, DP):
             partial_to(src, r).start()
 
@@ -186,28 +239,34 @@
         s = qbuf[src * DP].astype(F32)
         for p in range(1, DP):
             s = s + qbuf[src * DP + p].astype(F32)
-        w = xg[pl.ds(src * DP, DP)][:, :, rows:].astype(F32)[:, :T].reshape(DP * T, 128)
-        at = lax.broadcasted_iota(jnp.int32, (DP * T, 128), 1)
-        g = jnp.sum(jnp.where(at == my_expert, w, 0.0), axis=1, keepdims=True)
+        s = s[:slots]
+        diag = at_lane[:slots] == at_row[:slots]
+        g = jnp.sum(
+            jnp.where(diag, jnp.broadcast_to(shares[src][:1], (slots, 128)), 0.0),
+            axis=1, keepdims=True,
+        )
         gate, up, hg = s[:, :hd], s[:, hd : 2 * hd], s[:, 2 * hd :]
         sig = jax.nn.sigmoid(gate)
         act = gate * sig
-        hidden = jnp.where(g > 0.0, (act * up).astype(BF16).astype(F32), 0.0)
+        hidden = (act * up).astype(BF16).astype(F32)
         hidden_grad = g * hg
         gate_grad = hidden_grad * up * sig * (1.0 + gate * (1.0 - sig))
         up_grad = hidden_grad * act
         score = jnp.sum(hidden * hg, axis=1, keepdims=True)
-        ssend[src] = jnp.broadcast_to(score, (DP * T, 128)).reshape(DP, T, 128)
+        score_row = jnp.sum(jnp.where(diag, score, 0.0), axis=0, keepdims=True)
+        ssend[src] = jnp.broadcast_to(score_row, (8, 128))
         both = jnp.concatenate([gate_grad, up_grad], axis=1)
-        upper = jnp.concatenate([both, jnp.zeros_like(gate)], axis=1).reshape(DP, T, 3 * hd)
-        lower = jnp.concatenate([jnp.zeros_like(both), g * hidden], axis=1).reshape(DP, T, 3 * hd)
-        hbuf[pl.ds(src * DP, DP)] = jnp.concatenate([upper, lower], axis=1).astype(BF16)
+        upper = jnp.concatenate([both, jnp.zeros_like(gate)], axis=1)
+        lower = jnp.concatenate([jnp.zeros_like(both), g * hidden], axis=1)
+        hbuf[src] = jnp.concatenate([upper, lower], axis=0).astype(BF16)
         ig = lax.dot_general(
             both.astype(BF16), wcat[:, : 2 * hd], contract_last, preferred_element_type=F32
-        ).astype(BF16)
+        )
+        filler = jnp.zeros((padded - slots, rows), F32)
+        ig = jnp.concatenate([ig, filler], axis=0).astype(BF16)
         if own:
             igrecv[src] = ig
-            srecv[src] = ssend[src, d]
+            srecv[src] = ssend[src]
         else:
             igsend[src] = ig
             rows_back(src).start()
@@ -235,8 +294,8 @@
             finish(src, False)
 
     if E <= 4:
-        a = xg[...][:, :, :rows].reshape(E * DP * 2 * T, rows)
-        b = hbuf[...].reshape(E * DP * 2 * T, 3 * hd)
+        a = packed[...].reshape(E * 2 * slots, rows)
+        b = hbuf[...].reshape(E * 2 * slots, 3 * hd)
         grads = lax.dot_general(a, b, contract_first, preferred_element_type=F32)
         for i, ref in enumerate((gg_ref, gu_ref, gd_ref)):
             ref[0] = grads[:, i * hd : (i + 1) * hd]
@@ -246,8 +305,8 @@
 
         @pl.loop(0, E)
         def _(j):
-            a = xg[pl.ds(j * DP, DP)][:, :, :rows].reshape(DP * 2 * T, rows)
-            b = hbuf[pl.ds(j * DP, DP)].reshape(DP * 2 * T, 3 * hd)
+            a = packed[j].reshape(2 * slots, rows)
+            b = hbuf[j]
             grads = lax.dot_general(a, b, contract_first, preferred_element_type=F32)
             for i, ref in enumerate((gg_ref, gu_ref, gd_ref)):
                 ref[0] = ref[0] + grads[:, i * hd : (i + 1) * hd]
@@ -257,39 +316,65 @@
         score_in(other(r + 1)).wait_recv()
 
     loop(E - 1, await_back)
+    group = 128 // padded
+
+    def unpack(q):
+        block = q * group + at_lane // padded
+        place = jnp.zeros((count, 128), F32)
+        for j in range(experts):
+            hit = (at_lane % padded).astype(F32) == slot[:, j : j + 1]
+            hit = jnp.logical_and(hit, at_lane % padded < slots)
+            place = place + jnp.where(jnp.logical_and(hit, block // slices == j), 1.0, 0.0)
+        got = igrecv[pl.ds(q * group, group)].reshape(128, rows)
+        return jnp.dot(place.astype(BF16), got, preferred_element_type=F32)
+
     if E <= 4:
-        total = igrecv[0].astype(F32)
-        for j in range(1, E):
-            total = total + igrecv[j].astype(F32)
+        total = unpack(0)
     else:
         total = lax.fori_loop(
-            0, E, lambda j, t: t + igrecv[j].astype(F32), jnp.zeros((DP * T, rows), F32)
-        )
-    fsend[...] = total.reshape(DP, T, rows).astype(BF16)
+            0, E // group, lambda q, t: t + unpack(q), jnp.zeros((count, rows), F32)
+        )
+    fsend[...] = total.reshape(DP, 2 * T, rows)[:, :T].astype(BF16)
     for p in range(DP):
         hand_on(p).start()
 
+    tok_row = lax.broadcasted_iota(jnp.int32, (T, T), 0)
+    tok_col = lax.broadcasted_iota(jnp.int32, (T, T), 1)
+    tok_rank = jnp.dot(
+        jnp.where(tok_col < tok_row, 1.0, 0.0).astype(BF16),
+        jnp.where(weight > 0.0, 1.0, 0.0).astype(BF16),
+        preferred_element_type=F32,
+    )
+    tok_slot = tok_rank + (d * cap).astype(F32)
     for k in range(top):
-        out = jnp.zeros((T, 128), F32)
+        own_slot = jnp.sum(jnp.where(named[k] == lane, tok_slot, 0.0), axis=1, keepdims=True)
+        out = jnp.zeros((T, 1), F32)
         for j in range(E):
             if j % slices == 0:
                 per = srecv[j]
                 for m in range(1, slices):
                     per = per + srecv[j + m]
-                out = out + jnp.where(named[k] == j // slices, per, 0.0)
+                pick = jnp.sum(
+                    jnp.where(lane.astype(F32) == own_slot, per, 0.0), axis=1, keepdims=True
+                )
+                out = out + jnp.where(named[k] == j // slices, pick, 0.0)
         row = jnp.sum(jnp.where(diagonal, out, 0.0), axis=0, keepdims=True)
         gc_ref[0, k : k + 1, :] = row[:, :T]
 
     for r in range(1, DP):
         scatter(r).wait_send()
 
+    for k in range(1, experts):
+        for p in range(pieces + 1):
+            send_away(lax.rem(my_expert + k, experts), p).wait_send()
+
     def sent(i):
         src = source(i)
-        for r in range(DP):
+        for p in range(pieces + 1):
             for way in range(2):
                 @pl.when(going(src, way))
                 def _():
-                    relay(src, peer(r), way).wait_send()
+                    relay(src, p, way).wait_send()
         for r in range(1, DP):
             partial_to(src, r).wait_send()
 
@@ -327,6 +412,9 @@
         T, D = tokens.shape[1:]
         top = routes.shape[2]
         rows, hd = w_gate.shape[1:]
+        experts = E // slices
+        slots = DP * min(T, max(2, 3 * T * top // (2 * experts)))
+        pieces = 2 * slots // 16
         vmem = pl.BlockSpec(memory_space=pltpu.VMEM)
         hbm = pl.BlockSpec(memory_space=pltpu.HBM)
         dma = pltpu.SemaphoreType.DMA
@@ -347,17 +435,22 @@
                 pltpu.VMEM((1, top, T), jnp.int32),
                 pltpu.VMEM((1, top, T), BF16),
                 pltpu.VMEM((DP, 2 * T, rows + 128), BF16),
-                pltpu.VMEM((E * DP, 2 * T, rows + 128), BF16),
+                pltpu.VMEM((DP, 2 * T, rows + 128), BF16),
                 pltpu.VMEM((rows, 3 * hd), BF16),
+                pltpu.VMEM((E, pieces, 16, rows), BF16),
+                pltpu.VMEM((experts, pieces, 16, rows), BF16),
+                pltpu.VMEM((E, 8, 128), F32),
+                pltpu.VMEM((experts, 8, 128), F32),
                 pltpu.VMEM((E * DP, DP * T, 3 * hd), BF16),
-                pltpu.VMEM((E * DP, 2 * T, 3 * hd), BF16),
+                pltpu.VMEM((E, 2 * slots, 3 * hd), BF16),
                 pltpu.VMEM((E, DP * T, rows), BF16),
                 pltpu.VMEM((E, DP * T, rows), BF16),
-                pltpu.VMEM((E, DP, T, 128), F32),
-                pltpu.VMEM((E, T, 128), F32),
+                pltpu.VMEM((E, 8, 128), F32),
+                pltpu.VMEM((E, 8, 128), F32),
                 pltpu.VMEM((DP, T, rows), BF16),
                 pltpu.VMEM((DP, T, rows), BF16),
-                dma((4,)), dma((3,)), dma((DP,)), dma((E, DP)), dma((2, E, DP)),
+                dma((4,)), dma((3,)), dma((DP,)), dma((DP,)),
+                dma((experts, pieces + 1)), dma((E, pieces + 1)), dma((2, E, pieces + 1)),
                 dma((E, DP)), dma((E, DP)), dma((E,)), dma((E,)),
                 dma((E,)), dma((E,)), dma((DP,)), dma((DP,)),
             ],

time: 35.9 us -> 37.8 us (1.053)
  Pallas kernels: 35.1 us -> 37 us
    pallas_call x1, Pallas kernels: 34 us -> 35.8 us  [body(): pl.pallas_call(functools.partial(kernel, (pipes, E, DP, slices)), out_sha...]
where the time goes in v5:
time: 37.8 us; the launch traced here: 37.6 us
  Pallas kernels  37 us (98%)
  between operations  0.64 us (2%)
    pallas_call x1, Pallas kernels, body(): pl.pallas_call(functools.partial(kernel, (pipes, E, DP, slices)), out_sha...  35.8 us
    pallas_call x1, Pallas kernels, body(): pl.pallas_call(write_out, out_shape=shapes, in_specs=[vmem] * 5, out_spec...  1.14 us

profile of v5, /device:TPU:1, one launch (start us, length us, event | category | flops | bytes accessed | tf_op | source)
XLA Modules:
  0.0 37.6 jit_solution(13705387754187159362)
XLA Ops:
  0.6 35.8 %shard_map.110 = (bf16[1,8,3584]{2,1,0:T(8,128)(2,1)S(1)}, f32[1,1,8]{2,1,0:T(1,128)S(1)}, f32[1,896,128]{2,1,0:T(8,128)S(1)}, f32[1,896,128]{2,1,0:T(8,128)S(1)}, f32[1,896,128]{2,1,0:T(8,128)S(1)}) custom-call(bf16[1,8,3584]{2,1,0:T(8,128)(2,1)} %tok_hbm.1, bf16[1,8,3584]{2,1,0:T(8,128)(2,1)} %go_hbm.1, s32[1,1,8]{2,1,0:T(1,128)} %bitcast.3, ...), custom_call_target="tpu_custom_call" | custom-call | tf_op jit(solution)/shard_map/pallas_call | solution.py:427
  36.5 1.1 %shard_map.111 = (bf16[1,8,3584]{2,1,0:T(8,128)(2,1)}, f32[1,1,8]{2,1,0:T(1,128)}, f32[1,896,128]{2,1,0:T(8,128)}, f32[1,896,128]{2,1,0:T(8,128)}, f32[1,896,128]{2,1,0:T(8,128)}) custom-call(bf16[1,8,3584]{2,1,0:T(8,128)(2,1)S(1)} %get-tuple-element.15.refs_0_, f32[1,1,8]{2,1,0:T(1,128)S(1)} %get-tuple-element.16.refs_1_, ...), custom_call_target="tpu_custom_call" | custom-call | tf_op jit(solution)/shard_map/pallas_call | solution.py:469

commit v6 on v4

v6 whole, which is shorter than its diff:
```python
import functools

import jax
import jax.numpy as jnp
from jax import lax
from jax.experimental import pallas as pl
from jax.experimental.pallas import tpu as pltpu
from jax.sharding import PartitionSpec as P

MESH = pl.DeviceIdType.MESH
F32, BF16 = jnp.float32, jnp.bfloat16
contract_last = (((1,), (1,)), ((), ()))
contract_first = (((0,), (0,)), ((), ()))


def loop(count, step):
    if count <= 4:
        for i in range(count):
            step(i)
    else:
        pl.loop(0, count)(step)


def kernel(
    sizes, tok_hbm, go_hbm, routes_hbm, comb_hbm, wg_hbm, wu_hbm, wd_hbm,
    passed_ref, gc_ref, gg_ref, gu_ref, gd_ref,
    routes_ref, comb_ref, xg, wbuf, wcat, qbuf, h_in, h_out, igsend, ssend, srecv, frecv,
    isem, wsem, p1s, ws, wr, gr, zs, qs, qr, igs, ss, sr, fr,
):
    pipes, E, DP, slices = sizes
    T = tok_hbm.shape[1]
    top = routes_ref.shape[1]
    rows, hd = wg_hbm.shape[1:]
    pipe, e, d = (lax.axis_index(a) for a in ("pipe", "expert", "dp"))
    behind = lax.rem(pipe + pipes - 1, pipes)
    ahead = lax.rem(pipe + 1, pipes)
    my_expert = e // slices

    def peer(r):
        return lax.rem(d + r, DP)

    def other(r):
        return lax.rem(e + r, E)

    barrier = pltpu.get_barrier_semaphore()

    def greet(*who):
        pl.semaphore_signal(barrier, inc=1, device_id=who, device_id_type=MESH)

    loop(DP - 1, lambda r: greet(pipe, e, peer(r + 1)))
    loop(E - 1, lambda r: greet(pipe, other(r + 1), d))
    loop(E, lambda j: loop(DP, lambda r: greet(ahead, j, r)))

    def mine(ref, p):
        return ref.at[0, :, pl.ds(pl.multiple_of(p * rows, rows), rows)]

    home = e * DP + d
    given = [
        pltpu.make_async_copy(a, b, isem.at[i])
        for i, (a, b) in enumerate(
            (
                (mine(tok_hbm, d), xg.at[home, 0]), (mine(go_hbm, d), xg.at[home, 1]),
                (routes_hbm, routes_ref), (comb_hbm, comb_ref),
            )
        )
    ]
    for c in given:
        c.start()
    loads = [
        pltpu.make_async_copy(w.at[0], wcat.at[:, pl.ds(i * hd, hd)], wsem.at[i])
        for i, w in enumerate((wg_hbm, wu_hbm, wd_hbm))
    ]
    for c in loads:
        c.start()

    pl.semaphore_wait(barrier, DP - 1 + E - 1 + E * DP)

    def remote(src, dst, send, recv, who):
        return pltpu.make_async_remote_copy(
            src_ref=src, dst_ref=dst, send_sem=send, recv_sem=recv,
            device_id=who, device_id_type=MESH,
        )

    def scatter(r, i):
        to = peer(r)
        ref = (tok_hbm, go_hbm)[i]
        return remote(mine(ref, to), xg.at[home, i], p1s.at[r, i], gr.at[e, d], (pipe, e, to))

    def part(src, p):
        return wbuf.at[src] if p == DP else xg.at[src * DP + p]

    def weights_to(r):
        block = wbuf.at[e, d]
        return remote(block, block, ws.at[r], wr.at[d], (pipe, e, peer(r)))

    def weights_from(r):
        p = peer(r)
        block = wbuf.at[e, p]
        return remote(block, block, ws.at[r], wr.at[p], (pipe, e, p))

    def relay(src, p, way):
        block = part(src, p) if isinstance(p, int) else xg.at[src * DP + p]
        to = jnp.clip(e + (1 if way == 0 else -1), 0, E - 1)
        return remote(block, block, zs.at[way, src, p], gr.at[src, p], (pipe, to, d))

    def going(src, way):
        if way == 0:
            return jnp.logical_and(src <= e, e + 1 < E)
        return jnp.logical_and(src >= e, e > 0)

    def partial_to(src, r):
        block = qbuf.at[src * DP + d]
        return remote(block, block, qs.at[src, r], qr.at[src, d], (pipe, e, peer(r)))

    def partial_from(src, r):
        p = peer(r)
        block = qbuf.at[src * DP + p]
        return remote(block, block, qs.at[src, r], qr.at[src, p], (pipe, e, p))

    def rows_back(src, p):
        return remote(
            igsend.at[src, p], frecv.at[e, d], igs.at[src, p], fr.at[e, d], (behind, src, p)
        )

    def rows_in(src, p):
        return remote(
            igsend.at[src, p], frecv.at[src, p], igs.at[src, p], fr.at[src, p], (behind, src, p)
        )

    def score_back(src):
        return remote(ssend.at[src, d], srecv.at[e], ss.at[src], sr.at[e], (pipe, src, d))

    def score_in(src):
        return remote(ssend.at[src, d], srecv.at[src], ss.at[src], sr.at[src], (pipe, src, d))

    for r in range(1, DP):
        for i in range(2):
            scatter(r, i).start()

    lane = lax.broadcasted_iota(jnp.int32, (T, 128), 1)
    diagonal = lane == lax.broadcasted_iota(jnp.int32, (T, 128), 0)
    for c in given[2:]:
        c.wait()

    def column(row):
        spread = jnp.broadcast_to(row, (T, T))
        return jnp.sum(jnp.where(diagonal[:, :T], spread, 0), axis=1, keepdims=True)

    named = [column(routes_ref[0, k : k + 1, :]) for k in range(top)]
    weight = jnp.zeros((T, 128), F32)
    for k in range(top):
        share = column(comb_ref[0, k : k + 1, :].astype(F32))
        weight = weight + jnp.where(named[k] == lane, share, 0.0)
    wbuf[e, d] = weight
    for r in range(1, DP):
        weights_to(r).start()
    for c in given[:2]:
        c.wait()

    near = jnp.minimum(e, E - 1 - e)

    def source(i):
        half = (i + 1) // 2
        sign = jnp.where(i % 2 == 1, 1, -1)
        both_sides = e + sign * half
        one_side = jnp.where(e < E - 1 - e, e + (i - near), e - (i - near))
        return jnp.where(i <= 2 * near, both_sides, one_side)

    def arrive(i, first):
        src = e if first else source(i)

        def pass_on(p):
            for way in range(2):
                @pl.when(going(src, way))
                def _():
                    relay(src, p, way).start()

        for r in range(DP):
            if not (first and r == 0):
                relay(src, peer(r), 0).wait_recv()
            pass_on(peer(r))
        if first:
            for r in range(1, DP):
                weights_from(r).wait_recv()
        else:
            relay(src, DP, 0).wait_recv()
        pass_on(DP)
        return src

    def sides(src):
        blocks = xg[pl.ds(src * DP, DP)]
        return [blocks[:, i].reshape(DP * T, rows) for i in range(2)]

    def project(src):
        x, out = sides(src)
        q = jnp.concatenate(
            [
                jnp.dot(x, wcat[:, : 2 * hd], preferred_element_type=F32),
                jnp.dot(out, wcat[:, 2 * hd :], preferred_element_type=F32),
            ],
            axis=1,
        )
        qbuf[src * DP + d] = q.astype(BF16)
        for r in range(1, DP):
            partial_to(src, r).start()

    def finish(src, own):
        for r in range(1, DP):
            partial_from(src, r).wait_recv()
        s = qbuf[src * DP].astype(F32)
        for p in range(1, DP):
            s = s + qbuf[src * DP + p].astype(F32)
        w = wbuf[src].reshape(DP * T, 128)
        at = lax.broadcasted_iota(jnp.int32, (DP * T, 128), 1)
        g = jnp.sum(jnp.where(at == my_expert, w, 0.0), axis=1, keepdims=True)
        gate, up, hg = s[:, :hd], s[:, hd : 2 * hd], s[:, 2 * hd :]
        sig = jax.nn.sigmoid(gate)
        act = gate * sig
        hidden = jnp.where(g > 0.0, (act * up).astype(BF16).astype(F32), 0.0)
        hidden_grad = g * hg
        gate_grad = hidden_grad * up * sig * (1.0 + gate * (1.0 - sig))
        up_grad = hidden_grad * act
        score = jnp.sum(hidden * hg, axis=1, keepdims=True)
        ssend[src] = jnp.broadcast_to(score, (DP * T, 128)).reshape(DP, T, 128)
        both = jnp.concatenate([gate_grad, up_grad], axis=1)
        h_in[src] = both.astype(BF16)
        h_out[src] = (g * hidden).astype(BF16)
        ig = lax.dot_general(
            both.astype(BF16), wcat[:, : 2 * hd], contract_last, preferred_element_type=F32
        ).astype(BF16)
        igsend[src] = ig.reshape(DP, T, rows)
        for p in range(DP):
            rows_back(src, p).start()
        if own:
            srecv[src] = ssend[src, d]
        else:
            score_back(src).start()

    src = arrive(0, True)
    for c in loads:
        c.wait()
    project(src)
    last = src
    if E <= 4:
        for i in range(1, E):
            src = arrive(i, False)
            project(src)
            finish(last, i == 1)
            last = src
        finish(last, False)
    else:
        finish(src, True)

        @pl.loop(1, E)
        def _(i):
            src = arrive(i, False)
            project(src)
            finish(src, False)

    if E <= 4:
        blocks = xg[...]
        x, out = [blocks[:, i].reshape(E * DP * T, rows) for i in range(2)]
        inward = lax.dot_general(
            x, h_in[...].reshape(E * DP * T, 2 * hd), contract_first, preferred_element_type=F32
        )
        gg_ref[0] = inward[:, :hd]
        gu_ref[0] = inward[:, hd:]
        gd_ref[0] = lax.dot_general(
            out, h_out[...].reshape(E * DP * T, hd), contract_first, preferred_element_type=F32
        )
    else:
        for ref in (gg_ref, gu_ref, gd_ref):
            ref[0] = jnp.zeros((rows, hd), F32)

        @pl.loop(0, E)
        def _(j):
            x, out = sides(j)
            inward = lax.dot_general(x, h_in[j], contract_first, preferred_element_type=F32)
            gg_ref[0] = gg_ref[0] + inward[:, :hd]
            gu_ref[0] = gu_ref[0] + inward[:, hd:]
            gd_ref[0] = gd_ref[0] + lax.dot_general(
                out, h_out[j], contract_first, preferred_element_type=F32
            )

    loop(E - 1, lambda r: score_in(other(r + 1)).wait_recv())
    for k in range(top):
        out = jnp.zeros((T, 128), F32)
        for j in range(E):
            if j % slices == 0:
                per = srecv[j]
                for m in range(1, slices):
                    per = per + srecv[j + m]
                out = out + jnp.where(named[k] == j // slices, per, 0.0)
        row = jnp.sum(jnp.where(diagonal, out, 0.0), axis=0, keepdims=True)
        gc_ref[0, k : k + 1, :] = row[:, :T]

    for r in range(1, DP):
        for i in range(2):
            scatter(r, i).wait_send()
        weights_to(r).wait_send()

    def sent(i):
        src = source(i)
        for p in [peer(r) for r in range(DP)] + [DP]:
            for way in range(2):
                @pl.when(going(src, way))
                def _():
                    relay(src, p, way).wait_send()
        for p in range(DP):
            rows_back(src, p).wait_send()
        for r in range(1, DP):
            partial_to(src, r).wait_send()

    loop(E, sent)

    loop(E - 1, lambda r: score_back(other(r + 1)).wait_send())

    loop(E, lambda j: loop(DP, lambda p: rows_in(j, p).wait_recv()))
    for p in range(DP):
        if E <= 4:
            total = frecv[0, p].astype(F32)
            for j in range(1, E):
                total = total + frecv[j, p].astype(F32)
        else:
            total = lax.fori_loop(
                0, E, lambda j, t: t + frecv[j, p].astype(F32), jnp.zeros((T, rows), F32)
            )
        passed_ref[0, :, p * rows : (p + 1) * rows] = total.astype(BF16)


def write_out(*refs):
    count = len(refs) // 2
    sems = refs[-1]
    copies = [
        pltpu.make_async_copy(refs[i], refs[count + i], sems.at[i]) for i in range(count)
    ]
    for c in copies:
        c.start()
    for c in copies:
        c.wait()


def solution(mesh):
    pipes, E, DP = (mesh.shape[a] for a in ("pipe", "expert", "dp"))
    slices = min(8, E // 2)

    def body(tokens, grad_out, routes, combine, w_gate, w_up, w_down):
        T, D = tokens.shape[1:]
        top = routes.shape[2]
        rows, hd = w_gate.shape[1:]
        vmem = pl.BlockSpec(memory_space=pltpu.VMEM)
        hbm = pl.BlockSpec(memory_space=pltpu.HBM)
        dma = pltpu.SemaphoreType.DMA
        grad = jax.ShapeDtypeStruct((1, rows, hd), F32)
        shapes = (
            jax.ShapeDtypeStruct((1, T, D), BF16),
            jax.ShapeDtypeStruct((1, top, T), F32),
            grad, grad, grad,
        )
        results = pl.pallas_call(
            functools.partial(kernel, (pipes, E, DP, slices)),
            out_shape=shapes,
            in_specs=[hbm] * 7,
            out_specs=[vmem] * 5,
            scratch_shapes=[
                pltpu.VMEM((1, top, T), jnp.int32),
                pltpu.VMEM((1, top, T), BF16),
                pltpu.VMEM((E * DP, 2, T, rows), BF16),
                pltpu.VMEM((E, DP, T, 128), F32),
                pltpu.VMEM((rows, 3 * hd), BF16),
                pltpu.VMEM((E * DP, DP * T, 3 * hd), BF16),
                pltpu.VMEM((E, DP * T, 2 * hd), BF16),
                pltpu.VMEM((E, DP * T, hd), BF16),
                pltpu.VMEM((E, DP, T, rows), BF16),
                pltpu.VMEM((E, DP, T, 128), F32),
                pltpu.VMEM((E, T, 128), F32),
                pltpu.VMEM((E, DP, T, rows), BF16),
                dma((4,)), dma((3,)), dma((DP, 2)), dma((DP,)), dma((DP,)),
                dma((E, DP + 1)), dma((2, E, DP + 1)), dma((E, DP)), dma((E, DP)),
                dma((E, DP)), dma((E,)), dma((E,)), dma((E, DP)),
            ],
            compiler_params=pltpu.CompilerParams(
                collective_id=0, has_side_effects=True, vmem_limit_bytes=48 * 2**20
            ),
        )(
            *(
                pltpu.with_memory_space_constraint(a, pltpu.HBM)
                for a in (
                    tokens, grad_out, jnp.swapaxes(routes, 1, 2), jnp.swapaxes(combine, 1, 2),
                    w_gate, w_up, w_down,
                )
            )
        )
        passed, grad_combine, *grads = pl.pallas_call(
            write_out,
            out_shape=shapes,
            in_specs=[vmem] * 5,
            out_specs=[hbm] * 5,
            scratch_shapes=[dma((5,))],
            compiler_params=pltpu.CompilerParams(vmem_limit_bytes=2 * 2**20),
        )(*results)
        return (passed, jnp.swapaxes(grad_combine, 1, 2), *grads)

    weights = P("pipe", "dp", "expert")
    mine = P("pipe", ("expert", "dp"), None)
    return jax.shard_map(
        body, mesh=mesh, in_specs=(mine,) * 4 + (weights,) * 3,
        out_specs=(mine, mine, weights, weights, weights), check_vma=False,
    )
```

time: 35.9 us -> 34.9 us (0.972)
  the two profiles are of different devices: /device:TPU:1 before, /device:TPU:0 now
where the time goes in v6:
time: 34.9 us; the launch traced here: 34.8 us
  Pallas kernels  34.1 us (98%)
  between operations  0.64 us (2%)
    pallas_call x1, Pallas kernels, body(): pl.pallas_call(functools.partial(kernel, (pipes, E, DP, slices)), out_sha...  33 us
    pallas_call x1, Pallas kernels, body(): pl.pallas_call(write_out, out_shape=shapes, in_specs=[vmem] * 5, out_spec...  1.14 us

profile of v6, /device:TPU:0, one launch (start us, length us, event | category | flops | bytes accessed | tf_op | source)
XLA Modules:
  0.0 34.8 jit_solution(11663587520357053269)
XLA Ops:
  0.6 33.0 %shard_map.110 = (bf16[1,8,3584]{2,1,0:T(8,128)(2,1)S(1)}, f32[1,1,8]{2,1,0:T(1,128)S(1)}, f32[1,896,128]{2,1,0:T(8,128)S(1)}, f32[1,896,128]{2,1,0:T(8,128)S(1)}, f32[1,896,128]{2,1,0:T(8,128)S(1)}) custom-call(bf16[1,8,3584]{2,1,0:T(8,128)(2,1)} %tok_hbm.1, bf16[1,8,3584]{2,1,0:T(8,128)(2,1)} %go_hbm.1, s32[1,1,8]{2,1,0:T(1,128)} %bitcast.3, ...), custom_call_target="tpu_custom_call" | custom-call | tf_op jit(solution)/shard_map/pallas_call | solution.py:360
  33.6 1.1 %shard_map.111 = (bf16[1,8,3584]{2,1,0:T(8,128)(2,1)}, f32[1,1,8]{2,1,0:T(1,128)}, f32[1,896,128]{2,1,0:T(8,128)}, f32[1,896,128]{2,1,0:T(8,128)}, f32[1,896,128]{2,1,0:T(8,128)}) custom-call(bf16[1,8,3584]{2,1,0:T(8,128)(2,1)S(1)} %get-tuple-element.15.refs_0_, f32[1,1,8]{2,1,0:T(1,128)S(1)} %get-tuple-element.16.refs_1_, ...), custom_call_target="tpu_custom_call" | custom-call | tf_op jit(solution)/shard_map/pallas_call | solution.py:394

commit v7 on v6

--- a/solution.py
+++ b/solution.py
@@ -161,7 +161,7 @@
 
     def source(i):
         half = (i + 1) // 2
-        sign = jnp.where(i % 2 == 1, 1, -1)
+        sign = jnp.where(i % 2 == 1, 1, -1) * jnp.where(2 * e < E, -1, 1)
         both_sides = e + sign * half
         one_side = jnp.where(e < E - 1 - e, e + (i - near), e - (i - near))
         return jnp.where(i <= 2 * near, both_sides, one_side)
@@ -240,14 +240,17 @@
     for c in loads:
         c.wait()
     project(src)
-    last = src
     if E <= 4:
-        for i in range(1, E):
-            src = arrive(i, False)
-            project(src)
-            finish(last, i == 1)
-            last = src
-        finish(last, False)
+        near_by, far = range(1, min(E, 3)), range(3, E)
+        planes = [arrive(i, False) for i in near_by]
+        for plane in planes:
+            project(plane)
+        finish(src, True)
+        for i in far:
+            planes.append(arrive(i, False))
+            project(planes[-1])
+        for plane in planes:
+            finish(plane, False)
     else:
         finish(src, True)
 

time: 34.9 us -> 32.7 us (0.937)
  Pallas kernels: 34.1 us -> 31.9 us
    pallas_call x1, Pallas kernels: 33 us -> 30.8 us  [body(): pl.pallas_call(functools.partial(kernel, (pipes, E, DP, slices)), out_sha...]
where the time goes in v7:
time: 32.7 us; the launch traced here: 32.6 us
  Pallas kernels  31.9 us (98%)
  between operations  0.64 us (2%)
    pallas_call x1, Pallas kernels, body(): pl.pallas_call(functools.partial(kernel, (pipes, E, DP, slices)), out_sha...  30.8 us
    pallas_call x1, Pallas kernels, body(): pl.pallas_call(write_out, out_shape=shapes, in_specs=[vmem] * 5, out_spec...  1.14 us

profile of v7, /device:TPU:0, one launch (start us, length us, event | category | flops | bytes accessed | tf_op | source)
XLA Modules:
  0.0 32.6 jit_solution(198864546119080626)
XLA Ops:
  0.6 30.8 %shard_map.110 = (bf16[1,8,3584]{2,1,0:T(8,128)(2,1)S(1)}, f32[1,1,8]{2,1,0:T(1,128)S(1)}, f32[1,896,128]{2,1,0:T(8,128)S(1)}, f32[1,896,128]{2,1,0:T(8,128)S(1)}, f32[1,896,128]{2,1,0:T(8,128)S(1)}) custom-call(bf16[1,8,3584]{2,1,0:T(8,128)(2,1)} %tok_hbm.1, bf16[1,8,3584]{2,1,0:T(8,128)(2,1)} %go_hbm.1, s32[1,1,8]{2,1,0:T(1,128)} %bitcast.3, ...), custom_call_target="tpu_custom_call" | custom-call | tf_op jit(solution)/shard_map/pallas_call | solution.py:363
  31.4 1.1 %shard_map.111 = (bf16[1,8,3584]{2,1,0:T(8,128)(2,1)}, f32[1,1,8]{2,1,0:T(1,128)}, f32[1,896,128]{2,1,0:T(8,128)}, f32[1,896,128]{2,1,0:T(8,128)}, f32[1,896,128]{2,1,0:T(8,128)}) custom-call(bf16[1,8,3584]{2,1,0:T(8,128)(2,1)S(1)} %get-tuple-element.15.refs_0_, f32[1,1,8]{2,1,0:T(1,128)S(1)} %get-tuple-element.16.refs_1_, ...), custom_call_target="tpu_custom_call" | custom-call | tf_op jit(solution)/shard_map/pallas_call | solution.py:397

commit v8 on v7

--- a/solution.py
+++ b/solution.py
@@ -9,7 +9,6 @@
 
 MESH = pl.DeviceIdType.MESH
 F32, BF16 = jnp.float32, jnp.bfloat16
-contract_last = (((1,), (1,)), ((), ()))
 contract_first = (((0,), (0,)), ((), ()))
 
 
@@ -24,7 +23,7 @@
 def kernel(
     sizes, tok_hbm, go_hbm, routes_hbm, comb_hbm, wg_hbm, wu_hbm, wd_hbm,
     passed_ref, gc_ref, gg_ref, gu_ref, gd_ref,
-    routes_ref, comb_ref, xg, wbuf, wcat, qbuf, h_in, h_out, igsend, ssend, srecv, frecv,
+    routes_ref, comb_ref, xg, wbuf, wcat, flipped, qbuf, h_in, h_out, igsend, ssend, srecv, frecv,
     isem, wsem, p1s, ws, wr, gr, zs, qs, qr, igs, ss, sr, fr,
 ):
     pipes, E, DP, slices = sizes
@@ -98,15 +97,13 @@
         block = wbuf.at[e, p]
         return remote(block, block, ws.at[r], wr.at[p], (pipe, e, p))
 
-    def relay(src, p, way):
+    def give(p, to):
+        block = part(e, p) if isinstance(p, int) else xg.at[e * DP + p]
+        return remote(block, block, zs.at[to, p], gr.at[e, p], (pipe, to, d))
+
+    def shared(src, p):
         block = part(src, p) if isinstance(p, int) else xg.at[src * DP + p]
-        to = jnp.clip(e + (1 if way == 0 else -1), 0, E - 1)
-        return remote(block, block, zs.at[way, src, p], gr.at[src, p], (pipe, to, d))
-
-    def going(src, way):
-        if way == 0:
-            return jnp.logical_and(src <= e, e + 1 < E)
-        return jnp.logical_and(src >= e, e > 0)
+        return remote(block, block, zs.at[src, p], gr.at[src, p], (pipe, src, d))
 
     def partial_to(src, r):
         block = qbuf.at[src * DP + d]
@@ -170,20 +167,18 @@
         src = e if first else source(i)
 
         def pass_on(p):
-            for way in range(2):
-                @pl.when(going(src, way))
-                def _():
-                    relay(src, p, way).start()
+            if first:
+                loop(E - 1, lambda r: give(p, other(r + 1)).start())
 
         for r in range(DP):
             if not (first and r == 0):
-                relay(src, peer(r), 0).wait_recv()
+                shared(src, peer(r)).wait_recv()
             pass_on(peer(r))
         if first:
             for r in range(1, DP):
                 weights_from(r).wait_recv()
         else:
-            relay(src, DP, 0).wait_recv()
+            shared(src, DP).wait_recv()
         pass_on(DP)
         return src
 
@@ -225,8 +220,8 @@
         both = jnp.concatenate([gate_grad, up_grad], axis=1)
         h_in[src] = both.astype(BF16)
         h_out[src] = (g * hidden).astype(BF16)
-        ig = lax.dot_general(
-            both.astype(BF16), wcat[:, : 2 * hd], contract_last, preferred_element_type=F32
+        ig = jnp.dot(
+            both.astype(BF16), flipped[...], preferred_element_type=F32
         ).astype(BF16)
         igsend[src] = ig.reshape(DP, T, rows)
         for p in range(DP):
@@ -236,9 +231,10 @@
         else:
             score_back(src).start()
 
-    src = arrive(0, True)
     for c in loads:
         c.wait()
+    flipped[...] = wcat[:, : 2 * hd].T
+    src = arrive(0, True)
     project(src)
     if E <= 4:
         near_by, far = range(1, min(E, 3)), range(3, E)
@@ -304,17 +300,14 @@
 
     def sent(i):
         src = source(i)
-        for p in [peer(r) for r in range(DP)] + [DP]:
-            for way in range(2):
-                @pl.when(going(src, way))
-                def _():
-                    relay(src, p, way).wait_send()
         for p in range(DP):
             rows_back(src, p).wait_send()
         for r in range(1, DP):
             partial_to(src, r).wait_send()
 
     loop(E, sent)
+    for p in [peer(r) for r in range(DP)] + [DP]:
+        loop(E - 1, lambda r: give(p, other(r + 1)).wait_send())
 
     loop(E - 1, lambda r: score_back(other(r + 1)).wait_send())
 
@@ -371,6 +364,7 @@
                 pltpu.VMEM((E * DP, 2, T, rows), BF16),
                 pltpu.VMEM((E, DP, T, 128), F32),
                 pltpu.VMEM((rows, 3 * hd), BF16),
+                pltpu.VMEM((2 * hd, rows), BF16),
                 pltpu.VMEM((E * DP, DP * T, 3 * hd), BF16),
                 pltpu.VMEM((E, DP * T, 2 * hd), BF16),
                 pltpu.VMEM((E, DP * T, hd), BF16),
@@ -379,7 +373,7 @@
                 pltpu.VMEM((E, T, 128), F32),
                 pltpu.VMEM((E, DP, T, rows), BF16),
                 dma((4,)), dma((3,)), dma((DP, 2)), dma((DP,)), dma((DP,)),
-                dma((E, DP + 1)), dma((2, E, DP + 1)), dma((E, DP)), dma((E, DP)),
+                dma((E, DP + 1)), dma((E, DP + 1)), dma((E, DP)), dma((E, DP)),
                 dma((E, DP)), dma((E,)), dma((E,)), dma((E, DP)),
             ],
             compiler_params=pltpu.CompilerParams(

time: 32.7 us -> 35.7 us (1.092)
  Pallas kernels: 31.9 us -> 35 us
    pallas_call x1, Pallas kernels: 30.8 us -> 33.8 us  [body(): pl.pallas_call(functools.partial(kernel, (pipes, E, DP, slices)), out_sha...]
where the time goes in v8:
time: 35.7 us; the launch traced here: 35.6 us
  Pallas kernels  35 us (98%)
  between operations  0.64 us (2%)
    pallas_call x1, Pallas kernels, body(): pl.pallas_call(functools.partial(kernel, (pipes, E, DP, slices)), out_sha...  33.8 us
    pallas_call x1, Pallas kernels, body(): pl.pallas_call(write_out, out_shape=shapes, in_specs=[vmem] * 5, out_spec...  1.14 us

profile of v8, /device:TPU:0, one launch (start us, length us, event | category | flops | bytes accessed | tf_op | source)
XLA Modules:
  0.0 35.6 jit_solution(15208236306324670684)
XLA Ops:
  0.6 33.8 %shard_map.110 = (bf16[1,8,3584]{2,1,0:T(8,128)(2,1)S(1)}, f32[1,1,8]{2,1,0:T(1,128)S(1)}, f32[1,896,128]{2,1,0:T(8,128)S(1)}, f32[1,896,128]{2,1,0:T(8,128)S(1)}, f32[1,896,128]{2,1,0:T(8,128)S(1)}) custom-call(bf16[1,8,3584]{2,1,0:T(8,128)(2,1)} %tok_hbm.1, bf16[1,8,3584]{2,1,0:T(8,128)(2,1)} %go_hbm.1, s32[1,1,8]{2,1,0:T(1,128)} %bitcast.3, ...), custom_call_target="tpu_custom_call" | custom-call | tf_op jit(solution)/shard_map/pallas_call | solution.py:356
  34.5 1.1 %shard_map.111 = (bf16[1,8,3584]{2,1,0:T(8,128)(2,1)}, f32[1,1,8]{2,1,0:T(1,128)}, f32[1,896,128]{2,1,0:T(8,128)}, f32[1,896,128]{2,1,0:T(8,128)}, f32[1,896,128]{2,1,0:T(8,128)}) custom-call(bf16[1,8,3584]{2,1,0:T(8,128)(2,1)S(1)} %get-tuple-element.15.refs_0_, f32[1,1,8]{2,1,0:T(1,128)S(1)} %get-tuple-element.16.refs_1_, ...), custom_call_target="tpu_custom_call" | custom-call | tf_op jit(solution)/shard_map/pallas_call | solution.py:391

commit v9 on v7

--- a/solution.py
+++ b/solution.py
@@ -9,7 +9,6 @@
 
 MESH = pl.DeviceIdType.MESH
 F32, BF16 = jnp.float32, jnp.bfloat16
-contract_last = (((1,), (1,)), ((), ()))
 contract_first = (((0,), (0,)), ((), ()))
 
 
@@ -24,7 +23,7 @@
 def kernel(
     sizes, tok_hbm, go_hbm, routes_hbm, comb_hbm, wg_hbm, wu_hbm, wd_hbm,
     passed_ref, gc_ref, gg_ref, gu_ref, gd_ref,
-    routes_ref, comb_ref, xg, wbuf, wcat, qbuf, h_in, h_out, igsend, ssend, srecv, frecv,
+    routes_ref, comb_ref, xg, wbuf, wcat, flipped, qbuf, h_in, h_out, igsend, ssend, srecv, frecv,
     isem, wsem, p1s, ws, wr, gr, zs, qs, qr, igs, ss, sr, fr,
 ):
     pipes, E, DP, slices = sizes
@@ -179,6 +178,10 @@
             if not (first and r == 0):
                 relay(src, peer(r), 0).wait_recv()
             pass_on(peer(r))
+            if first and r == 0:
+                for c in loads:
+                    c.wait()
+                flipped[...] = wcat[:, : 2 * hd].T
         if first:
             for r in range(1, DP):
                 weights_from(r).wait_recv()
@@ -225,8 +228,8 @@
         both = jnp.concatenate([gate_grad, up_grad], axis=1)
         h_in[src] = both.astype(BF16)
         h_out[src] = (g * hidden).astype(BF16)
-        ig = lax.dot_general(
-            both.astype(BF16), wcat[:, : 2 * hd], contract_last, preferred_element_type=F32
+        ig = jnp.dot(
+            both.astype(BF16), flipped[...], preferred_element_type=F32
         ).astype(BF16)
         igsend[src] = ig.reshape(DP, T, rows)
         for p in range(DP):
@@ -237,8 +240,6 @@
             score_back(src).start()
 
     src = arrive(0, True)
-    for c in loads:
-        c.wait()
     project(src)
     if E <= 4:
         near_by, far = range(1, min(E, 3)), range(3, E)
@@ -371,6 +372,7 @@
                 pltpu.VMEM((E * DP, 2, T, rows), BF16),
                 pltpu.VMEM((E, DP, T, 128), F32),
                 pltpu.VMEM((rows, 3 * hd), BF16),
+                pltpu.VMEM((2 * hd, rows), BF16),
                 pltpu.VMEM((E * DP, DP * T, 3 * hd), BF16),
                 pltpu.VMEM((E, DP * T, 2 * hd), BF16),
                 pltpu.VMEM((E, DP * T, hd), BF16),

time: 32.7 us -> 32.7 us (level)
  no operation moved by 1% of the time
where the time goes in v9:
time: 32.7 us; the launch traced here: 32.5 us
  Pallas kernels  31.9 us (98%)
  between operations  0.64 us (2%)
    pallas_call x1, Pallas kernels, body(): pl.pallas_call(functools.partial(kernel, (pipes, E, DP, slices)), out_sha...  30.7 us
    pallas_call x1, Pallas kernels, body(): pl.pallas_call(write_out, out_shape=shapes, in_specs=[vmem] * 5, out_spec...  1.14 us

profile of v9, /device:TPU:0, one launch (start us, length us, event | category | flops | bytes accessed | tf_op | source)
XLA Modules:
  0.0 32.5 jit_solution(17587264226308831022)
XLA Ops:
  0.6 30.7 %shard_map.110 = (bf16[1,8,3584]{2,1,0:T(8,128)(2,1)S(1)}, f32[1,1,8]{2,1,0:T(1,128)S(1)}, f32[1,896,128]{2,1,0:T(8,128)S(1)}, f32[1,896,128]{2,1,0:T(8,128)S(1)}, f32[1,896,128]{2,1,0:T(8,128)S(1)}) custom-call(bf16[1,8,3584]{2,1,0:T(8,128)(2,1)} %tok_hbm.1, bf16[1,8,3584]{2,1,0:T(8,128)(2,1)} %go_hbm.1, s32[1,1,8]{2,1,0:T(1,128)} %bitcast.3, ...), custom_call_target="tpu_custom_call" | custom-call | tf_op jit(solution)/shard_map/pallas_call | solution.py:364
  31.4 1.1 %shard_map.111 = (bf16[1,8,3584]{2,1,0:T(8,128)(2,1)}, f32[1,1,8]{2,1,0:T(1,128)}, f32[1,896,128]{2,1,0:T(8,128)}, f32[1,896,128]{2,1,0:T(8,128)}, f32[1,896,128]{2,1,0:T(8,128)}) custom-call(bf16[1,8,3584]{2,1,0:T(8,128)(2,1)S(1)} %get-tuple-element.15.refs_0_, f32[1,1,8]{2,1,0:T(1,128)S(1)} %get-tuple-element.16.refs_1_, ...), custom_call_target="tpu_custom_call" | custom-call | tf_op jit(solution)/shard_map/pallas_call | solution.py:399
